TPU v7x, 512 devices: a whole 4x8x8 slice. The times are simulated.
512 devices in a mesh: seq: 64 (over y_hi, z, core), tensor: 8 (over x, y_lo).
Axes of the slice: x: 4, y: 8 (y_hi: 4, y_lo: 2; y = y_hi * 2 + y_lo), z: 8, core: 2. Of those that a mesh axis runs over, the one named last changes fastest.
Arguments:
- embedded: bfloat16 [16384, 4, 2048], P('seq', None, 'tensor'), may hold values from -6 to 6
- delays: int32 [4], replicated, may hold values from 0 to 3, each once
- norm_gain: float32 [2048], replicated, may hold values from 0.1 to 1.9
- w_query: bfloat16 [2048, 2048], P('seq', 'tensor'), may hold values from -0.125 to 0.125
- w_key: bfloat16 [2048, 2048], P('seq', 'tensor'), may hold values from -0.125 to 0.125
- w_value: bfloat16 [2048, 2048], P('seq', 'tensor'), may hold values from -0.125 to 0.125
- w_out: bfloat16 [2048, 2048], P('tensor', 'seq'), may hold values from -0.75 to 0.75
- text_states: bfloat16 [128, 768], P('seq'), may hold values from -6 to 6
- w_text_key: bfloat16 [768, 2048], P('seq', 'tensor'), may hold values from -0.21875 to 0.21875
- w_text_value: bfloat16 [768, 2048], P('seq', 'tensor'), may hold values from -0.21875 to 0.21875
- text_len: int32 [1], replicated, may hold values from 64 to 128
- cotangent: bfloat16 [16384, 2048], P('seq'), may hold values from -16 to 16
Outputs:
- attn_out: bfloat16 [16384, 2048], P('seq', 'tensor')
- d_embedded: bfloat16 [16384, 4, 2048], P('seq', None, 'tensor')
- d_wo: float32 [2048, 2048], P('tensor', 'seq')
- d_wtk: float32 [768, 2048], P('seq', 'tensor')
- d_wtv: float32 [768, 2048], P('seq', 'tensor')
Inputs may be any that keep to these rules, and one draw needn't show every extreme that they name: `delays`: each of 0 to 3 appears once. Text tokens with index text_len[0] or more are padding.
All inputs are finite; a program needn't handle non-finite values.
Results may differ from a plain program's by a relative error of at most 0.023.
Values may be sent and summed in bfloat16 or wider, within the bound.
A program may use at most 128 MiB of HBM per device.

v0:
```python
import jax
import jax.numpy as jnp
from jax import lax
from jax.sharding import PartitionSpec as P

HD = 64
WINDOW = 1500


EPS = 1e-05


def from_behind(block, axis, distance):
    devices = range(lax.axis_size(axis))
    route = [(i - distance, i) for i in devices if i - distance in devices]
    return lax.ppermute(block, axis, route)


def norm_forward(frames_in):
    widened = frames_in.astype(jnp.float32)
    row_mean = jnp.mean(widened, -1, keepdims=True)
    centred = widened - row_mean
    inv_std = lax.rsqrt(jnp.mean(centred * centred, -1, keepdims=True) + EPS)
    return (centred * inv_std, inv_std)


def contract_rows(left, right):
    return lax.dot_general(
        left, right, (((0,), (0,)), ((), ())), preferred_element_type=jnp.float32
    )


def contract_cols(left, right):
    return lax.dot_general(
        left, right, (((1,), (1,)), ((), ())), preferred_element_type=jnp.float32
    )


def shards(
    embedded,
    delays,
    norm_gain,
    w_query,
    w_key,
    w_value,
    w_out,
    text_states,
    w_text_key,
    w_text_value,
    text_len,
    cotangent,
):
    frames = embedded.shape[0]
    book_count = embedded.shape[1]
    local_cols = embedded.shape[2]
    full_width = local_cols * lax.axis_size("tensor")
    heads_here = local_cols // HD
    block_reach = (WINDOW + frames - 2) // frames
    key_lead = block_reach * frames
    key_extent = key_lead + frames
    seq_index = lax.axis_index("seq")
    col_first = lax.axis_index("tensor") * local_cols
    score_scale = HD ** (-0.5)
    lower_rim = from_behind(embedded[frames - (book_count - 1) :], "seq", 1)
    extended = jnp.concatenate([lower_rim, embedded], 0)
    summed = jnp.zeros((frames, local_cols), jnp.float32)
    for codebook in range(book_count):
        offset = book_count - 1 - delays[codebook]
        summed = summed + lax.dynamic_slice_in_dim(extended[:, codebook], offset, frames, 0).astype(
            jnp.float32
        )
    frames_local = summed.astype(jnp.bfloat16)
    frames_full = lax.all_gather(frames_local, "tensor", axis=1, tiled=True)
    unit_rows, inv_std = norm_forward(frames_full)
    normed = (unit_rows * norm_gain).astype(jnp.bfloat16)
    stacked = jnp.stack((w_query, w_key, w_value))
    full_proj, full_out = (
        lax.all_gather(stacked, "seq", axis=1, tiled=True),
        lax.all_gather(w_out, "seq", axis=1, tiled=True),
    )
    projected = jnp.einsum("fd,kdc->kfc", normed, full_proj, preferred_element_type=jnp.float32)
    projected = projected.astype(jnp.bfloat16)
    queries = projected[0]
    keys_own = projected[1]
    values_own = projected[2]
    states_all, text_kweight, text_vweight = (
        lax.all_gather(text_states, "seq", axis=0, tiled=True),
        lax.all_gather(w_text_key, "seq", axis=0, tiled=True),
        lax.all_gather(w_text_value, "seq", axis=0, tiled=True),
    )
    text_keys = jnp.dot(states_all, text_kweight, preferred_element_type=jnp.float32).astype(
        jnp.bfloat16
    )
    text_values = jnp.dot(states_all, text_vweight, preferred_element_type=jnp.float32).astype(
        jnp.bfloat16
    )
    text_total = states_all.shape[0]
    earlier = []
    for offset in range(1, block_reach + 1):
        earlier.append(from_behind((keys_own, values_own), "seq", offset))
    key_rows = jnp.concatenate([pair[0] for pair in reversed(earlier)] + [keys_own], 0)
    value_rows = jnp.concatenate([pair[1] for pair in reversed(earlier)] + [values_own], 0)
    row_ids = lax.broadcasted_iota(jnp.int32, (frames, key_extent), 0)
    col_ids = lax.broadcasted_iota(jnp.int32, (frames, key_extent), 1)
    distance = row_ids + key_lead - col_ids
    key_mask = (
        (distance >= 0) & (distance < WINDOW) & (seq_index * frames - key_lead + col_ids >= 0)
    )
    text_mask = lax.broadcasted_iota(jnp.int32, (frames, text_total), 1) < text_len[0]
    attended_heads = []
    kept_stats = []
    for head_index in range(heads_here):
        head_cols = slice(head_index * HD, (head_index + 1) * HD)
        q_head = queries[:, head_cols]
        scores = contract_cols(q_head, key_rows[:, head_cols]) * score_scale
        text_scores = contract_cols(q_head, text_keys[:, head_cols]) * score_scale
        weights = jnp.where(key_mask, jnp.exp(scores), 0.0)
        text_weights = jnp.where(text_mask, jnp.exp(text_scores), 0.0)
        totals = jnp.sum(weights, 1) + jnp.sum(text_weights, 1)
        mixture = jnp.dot(
            weights.astype(jnp.bfloat16),
            value_rows[:, head_cols],
            preferred_element_type=jnp.float32,
        )
        mixture = mixture + jnp.dot(
            text_weights.astype(jnp.bfloat16),
            text_values[:, head_cols],
            preferred_element_type=jnp.float32,
        )
        attended_heads.append((mixture / totals[:, None]).astype(jnp.bfloat16))
        kept_stats.append((weights, text_weights, totals))
    attended_output = jnp.concatenate(attended_heads, 1)
    out_partial = jnp.dot(attended_output, full_out, preferred_element_type=jnp.float32)
    out_grad = contract_cols(cotangent, full_out).astype(jnp.bfloat16)
    attn_local = lax.psum_scatter(
        out_partial.astype(jnp.bfloat16), "tensor", scatter_dimension=1, tiled=True
    )
    out_weight_grad = lax.psum_scatter(
        contract_rows(cotangent, attended_output), "seq", scatter_dimension=0, tiled=True
    )
    grads_q = []
    grads_k = []
    grads_v = []
    grads_tk = []
    grads_tv = []
    inner_list = []
    for head_index in range(heads_here):
        head_cols = slice(head_index * HD, (head_index + 1) * HD)
        weights, text_weights, totals = kept_stats[head_index]
        q_head = queries[:, head_cols]
        d_head = out_grad[:, head_cols]
        inner_dot = jnp.sum(
            d_head.astype(jnp.float32) * attended_heads[head_index].astype(jnp.float32), 1
        )
        inner_list.append(inner_dot)
        shares = weights / totals[:, None]
        text_shares = text_weights / totals[:, None]
        value_dots = contract_cols(d_head, value_rows[:, head_cols])
        text_dots = contract_cols(d_head, text_values[:, head_cols])
        grad_scores = (shares * (value_dots - inner_dot[:, None])).astype(jnp.bfloat16)
        text_grad_scores = (text_shares * (text_dots - inner_dot[:, None])).astype(jnp.bfloat16)
        grad_head = jnp.dot(grad_scores, key_rows[:, head_cols], preferred_element_type=jnp.float32)
        grad_head = grad_head + jnp.dot(
            text_grad_scores, text_keys[:, head_cols], preferred_element_type=jnp.float32
        )
        grads_q.append((grad_head * score_scale).astype(jnp.bfloat16))
        grads_k.append(contract_rows(grad_scores, q_head) * score_scale)
        grads_v.append(contract_rows(shares.astype(jnp.bfloat16), d_head))
        grads_tk.append(contract_rows(text_grad_scores, q_head) * score_scale)
        grads_tv.append(contract_rows(text_shares.astype(jnp.bfloat16), d_head))
    grad_queries = jnp.concatenate(grads_q, 1)
    key_partial = jnp.concatenate(grads_k, 1)
    value_partial = jnp.concatenate(grads_v, 1)
    key_grad = key_partial[key_lead:]
    value_grad = value_partial[key_lead:]
    for offset in range(1, block_reach + 1):
        lower = (block_reach - offset) * frames
        back_keys, back_values = (
            from_behind(
                key_partial[lower : lower + frames].astype(jnp.bfloat16), "seq", -offset
            ).astype(jnp.float32),
            from_behind(
                value_partial[lower : lower + frames].astype(jnp.bfloat16), "seq", -offset
            ).astype(jnp.float32),
        )
        key_grad = key_grad + back_keys
        value_grad = value_grad + back_values
    key_grad = key_grad.astype(jnp.bfloat16)
    value_grad = value_grad.astype(jnp.bfloat16)
    text_key_sum, text_value_sum = lax.psum(
        (jnp.concatenate(grads_tk, 1), jnp.concatenate(grads_tv, 1)), "seq"
    )
    feature_rows = w_text_key.shape[0]
    states_mine = lax.dynamic_slice_in_dim(states_all, seq_index * feature_rows, feature_rows, 1)
    d_wtk = contract_rows(states_mine, text_key_sum.astype(jnp.bfloat16))
    d_wtv = contract_rows(states_mine, text_value_sum.astype(jnp.bfloat16))
    grads_stack = jnp.stack((grad_queries, key_grad, value_grad))
    input_partial = jnp.einsum(
        "kfc,kdc->fd", grads_stack, full_proj, preferred_element_type=jnp.float32
    )
    input_grad = lax.psum_scatter(
        input_partial.astype(jnp.bfloat16), "tensor", scatter_dimension=1, tiled=True
    ).astype(jnp.float32)
    gain_local = lax.dynamic_slice_in_dim(norm_gain, col_first, local_cols, 0)
    unit_local = lax.dynamic_slice_in_dim(unit_rows, col_first, local_cols, 1)
    scaled = input_grad * gain_local
    plain_sum, unit_sum = lax.psum((jnp.sum(scaled, 1), jnp.sum(scaled * unit_local, 1)), "tensor")
    frame_grad = inv_std * (
        scaled - plain_sum[:, None] / full_width - unit_local * (unit_sum[:, None] / full_width)
    )
    frame_grad = frame_grad.astype(jnp.bfloat16)
    upper_rim = from_behind(frame_grad[: book_count - 1], "seq", -1)
    grad_extended = jnp.concatenate([frame_grad, upper_rim], 0)
    d_embedded = jnp.stack(
        [
            lax.dynamic_slice_in_dim(grad_extended, delays[codebook], frames, 0)
            for codebook in range(book_count)
        ],
        1,
    )
    return (attn_local, d_embedded, out_weight_grad.T, d_wtk, d_wtv)


def solution(mesh):
    placed = (
        P("seq", None, "tensor"),
        P(),
        P(),
        P("seq", "tensor"),
        P("seq", "tensor"),
        P("seq", "tensor"),
        P("tensor", "seq"),
        P("seq", None),
        P("seq", "tensor"),
        P("seq", "tensor"),
        P(),
        P("seq", None),
    )
    return jax.shard_map(
        shards,
        mesh=mesh,
        in_specs=placed,
        out_specs=(
            P("seq", "tensor"),
            P("seq", None, "tensor"),
            P("tensor", "seq"),
            P("seq", "tensor"),
            P("seq", "tensor"),
        ),
        check_vma=False,
    )
```

profile of v0, /device:TPU:33, one launch (start us, length us, event | category | flops | bytes accessed | tf_op | source)
XLA Modules:
  0.0 784.5 jit_solution(16173031977176931976)
XLA Ops:
  7.3 1.2 copy.34
  8.5 4.6 collective-permute-start
  22.4 83.4 %all-gather.1 = bf16[64,2,768]{2,1,0:T(2,128)(2,1)S(1)} all-gather(bf16[1,2,768]{2,1,0:T(2,128)(2,1)S(1)} %bitcast.96), channel_id=1, replica_groups=mesh['seq'=64,'tensor'=8] {'seq'}, dimensions={0}, use_global_device_ids=true | all-gather | bytes 199680 | tf_op jit(solution)/shard_map/all_gather | solution.py:87
  106.0 78.5 %all-gather.2 = bf16[64,12,256]{2,1,0:T(8,128)(2,1)S(1)} all-gather(bf16[1,12,256]{2,1,0:T(8,128)(2,1)S(1)} %bitcast.94), channel_id=1, replica_groups=mesh['seq'=64,'tensor'=8] {'seq'}, dimensions={0}, use_global_device_ids=true | all-gather | bytes 399360 | tf_op jit(solution)/shard_map/all_gather | solution.py:88
  184.6 80.5 %all-gather.3 = bf16[64,12,256]{2,1,0:T(8,128)(2,1)S(1)} all-gather(bf16[1,12,256]{2,1,0:T(8,128)(2,1)S(1)} %bitcast.95), channel_id=1, replica_groups=mesh['seq'=64,'tensor'=8] {'seq'}, dimensions={0}, use_global_device_ids=true | all-gather | bytes 399360 | tf_op jit(solution)/shard_map/all_gather | solution.py:89
  265.7 1.4 convert_reduce_fusion
  267.2 1.7 fusion.20
  269.0 1.7 convolution_convert_fusion.2
  270.8 3.0 fusion.25
  273.8 1.9 collective-permute-start.12
  275.8 1.9 collective-permute-start.11
  277.7 1.9 collective-permute-start.10
  279.6 1.9 collective-permute-start.7
  282.4 1.9 collective-permute-start.1
  285.3 24.4 %collective-permute-done.1 = bf16[256,256]{0,1:T(8,128)(2,1)S(1)} collective-permute-done((bf16[256,256]{0,1:T(8,128)(2,1)S(1)}, bf16[256,256]{0,1:T(8,128)(2,1)S(1)}, u32[]{:S(2)}, u32[]{:S(2)}) %collective-permute-start.1) | collective-permute-done | bytes 131104 | tf_op jit(solution)/shard_map/ppermute | solution.py:16
  309.7 1.9 collective-permute-start.2
  311.7 1.9 collective-permute-start.3
  313.6 13.6 %collective-permute-done.2 = bf16[256,256]{0,1:T(8,128)(2,1)S(1)} collective-permute-done((bf16[256,256]{0,1:T(8,128)(2,1)S(1)}, bf16[256,256]{0,1:T(8,128)(2,1)S(1)}, u32[]{:S(2)}, u32[]{:S(2)}) %collective-permute-start.2) | collective-permute-done | bytes 131104 | tf_op jit(solution)/shard_map/ppermute | solution.py:16
  327.2 4.5 collective-permute-start.4
  331.7 3.8 collective-permute-start.5
  335.5 5.1 collective-permute-done.4
  340.6 3.6 collective-permute-start.6
  344.2 1.0 collective-permute-done.5
  345.2 1.9 collective-permute-start.8
  347.1 2.1 collective-permute-start.9
  349.2 9.5 %collective-permute-done.8 = bf16[256,256]{0,1:T(8,128)(2,1)S(1)} collective-permute-done((bf16[256,256]{0,1:T(8,128)(2,1)S(1)}, bf16[256,256]{0,1:T(8,128)(2,1)S(1)}, u32[]{:S(2)}, u32[]{:S(2)}) %collective-permute-start.8) | collective-permute-done | bytes 131104 | tf_op jit(solution)/shard_map/ppermute | solution.py:16
  358.7 3.7 collective-permute-done.9
  362.5 1.0 fusion.203
  363.5 1.0 fusion.205
  364.5 1.0 fusion.207
  365.5 1.0 fusion.209
  369.4 1.0 multiply_reduce_fusion.4
  377.2 4.5 collective-permute-start.13
  381.6 1.9 collective-permute-start.18
  383.5 2.0 collective-permute-start.17
  385.5 1.9 collective-permute-start.16
  387.5 1.9 collective-permute-start.15
  389.7 3.0 collective-permute-start.14
  392.7 6.0 collective-permute-done.18
  398.8 3.4 collective-permute-start.19
  402.7 6.6 collective-permute-start.24
  409.3 5.5 collective-permute-start.23
  414.8 3.9 collective-permute-done.15
  418.7 1.9 collective-permute-start.22
  420.6 1.0 collective-permute-done.14
  421.6 3.4 collective-permute-start.21
  425.1 4.3 collective-permute-done.19
  429.4 2.6 collective-permute-start.20
  432.1 2.4 collective-permute-done.23
  434.5 3.0 collective-permute-done.22
  437.6 1.9 collective-permute-done.21
  439.5 2.9 collective-permute-done.20
  442.5 2.1 fusion.12
  444.9 2.3 convolution_convert_fusion
  456.1 1.7 fusion.18
  457.7 1.2 convolution_bitcast_fusion
  458.9 1.8 copy.48
  460.8 1.1 fusion.120
  463.5 276.7 %all-reduce.3 = (bf16[128,256]{0,1:T(8,128)(2,1)S(1)}, bf16[128,256]{0,1:T(8,128)(2,1)S(1)}) all-reduce(f32[128,256]{0,1:T(8,128)S(1)} %pad_maximum_fusion.4, f32[128,256]{0,1:T(8,128)S(1)} %pad_maximum_fusion.5), channel_id=1, replica_groups=mesh['seq'=64,'tensor'=8] {'seq'}, use_global_device_ids=true, to_apply=%region_21.22 | all-reduce | flops 65536 | bytes 393216 | tf_op jit(solution)/shard_map/psum | solution.py:190
  741.0 1.2 fusion.90
  742.2 19.4 %all-reduce.1 = (f32[256]{0:T(256)S(1)}, f32[256]{0:T(256)S(1)}) all-reduce(f32[256]{0:T(256)S(1)} %get-tuple-element.21, f32[256]{0:T(256)S(1)} %get-tuple-element.20), channel_id=1, replica_groups=mesh['seq'=64,'tensor'=8] {'tensor'}, use_global_device_ids=true, to_apply=%region_19.20 | all-reduce | flops 512 | bytes 4096 | tf_op jit(solution)/shard_map/psum | solution.py:207
  761.6 1.2 multiply_convert_fusion.1
  762.8 12.2 %collective-permute-start.25 = (bf16[3,256]{1,0:T(4,128)(2,1)S(1)}, bf16[3,256]{1,0:T(4,128)(2,1)S(1)}, u32[]{:S(2)}, u32[]{:S(2)}) collective-permute-start(bf16[3,256]{1,0:T(4,128)(2,1)S(1)} %slice.288), channel_id=1, source_target_pairs={{8,0},{16,8},{24,16},{32,24},{40,32},{48,40},{56,48},{64,56},{72,6... | collective-permute-start | bytes 4616 | tf_op jit(solution)/shard_map/ppermute | solution.py:16
  776.4 1.2 copy.41
  (198 shorter events, 21.1 us)
Async XLA Ops:
  7.2 261.8 %copy-start = (bf16[256,2048]{1,0:T(8,128)(2,1)S(1)}, bf16[256,2048]{1,0:T(8,128)(2,1)}, u32[]{:S(2)}) copy-start(bf16[256,2048]{1,0:T(8,128)(2,1)} %param.23) | copy-start | bytes 3145732
  7.2 6.0 copy-start.27
  7.2 13.8 %copy-start.22 = (bf16[32,256]{1,0:T(8,128)(2,1)S(1)}, bf16[32,256]{1,0:T(8,128)(2,1)}, u32[]{:S(2)}) copy-start(bf16[32,256]{1,0:T(8,128)(2,1)} %param.17) | copy-start | bytes 49156
  7.2 13.8 %copy-start.23 = (bf16[32,256]{1,0:T(8,128)(2,1)S(1)}, bf16[32,256]{1,0:T(8,128)(2,1)}, u32[]{:S(2)}) copy-start(bf16[32,256]{1,0:T(8,128)(2,1)} %param.16) | copy-start | bytes 49156
  7.2 13.8 %copy-start.24 = (bf16[32,256]{1,0:T(8,128)(2,1)S(1)}, bf16[32,256]{1,0:T(8,128)(2,1)}, u32[]{:S(2)}) copy-start(bf16[32,256]{1,0:T(8,128)(2,1)} %param.15) | copy-start | bytes 49156
  7.2 258.5 %all-gather.12.cloned.1.call-start = ((), (), s32[]{:S(2)}) async-start(), calls=%async_computation.7 | async-start | bytes 1179648 | tf_op jit(solution)/shard_map/all_gather | solution.py:73
  8.5 14.0 %copy-start.34 = (bf16[2,768]{1,0:T(2,128)(2,1)S(1)}, bf16[2,768]{1,0:T(2,128)(2,1)}, u32[]{:S(2)}) copy-start(bf16[2,768]{1,0:T(2,128)(2,1)} %param.19) | copy-start | bytes 9220
  8.5 97.5 %copy-start.25 = (bf16[12,256]{1,0:T(8,128)(2,1)S(1)}, bf16[12,256]{1,0:T(8,128)(2,1)}, u32[]{:S(2)}) copy-start(bf16[12,256]{1,0:T(8,128)(2,1)} %param.20) | copy-start | bytes 18436
  8.5 10.7 %collective-permute-start = (bf16[3,4,256]{2,0,1:T(4,128)(2,1)S(1)}, bf16[3,4,256]{2,0,1:T(4,128)(2,1)S(1)}, u32[]{:S(2)}, u32[]{:S(2)}) collective-permute-start(bf16[3,4,256]{2,0,1:T(4,128)(2,1)S(1)} %slice.240), channel_id=1, source_target_pairs={{0,8},{8,16},{16,24},{24,32},{32,40},{40,48},{48,56},{56,64},{64,7... | collective-permute-start | bytes 18440 | tf_op jit(solution)/shard_map/ppermute | solution.py:16
  19.3 165.3 %copy-start.26 = (bf16[12,256]{1,0:T(8,128)(2,1)S(1)}, bf16[12,256]{1,0:T(8,128)(2,1)}, u32[]{:S(2)}) copy-start(bf16[12,256]{1,0:T(8,128)(2,1)} %param.21) | copy-start | bytes 18436
  20.2 248.7 %all-gather.10.cloned.1.call-start = ((), (), s32[]{:S(2)}) async-start(), calls=%async_computation.4 | async-start | bytes 1064960 | tf_op jit(solution)/shard_map/all_gather | solution.py:79
  21.0 249.8 %all-gather.8.cloned.1.call-start = ((), (), s32[]{:S(2)}) async-start(), calls=%async_computation.3 | async-start | bytes 3194880 | tf_op jit(solution)/shard_map/all_gather | solution.py:78
  21.7 719.3 %reduce-scatter.8.cloned.1.call-start = ((), (), s32[]{:S(2)}) async-start(), calls=%async_computation.6 | async-start | bytes 1179648 | tf_op jit(solution)/shard_map/reduce_scatter | solution.py:201
  267.2 3.6 copy-start.1
  267.2 3.6 copy-start.35
  270.7 95.8 %copy-start.12 = (bf16[256,256]{0,1:T(8,128)(2,1)}, bf16[256,256]{0,1:T(8,128)(2,1)S(1)}, u32[]{:S(2)}) copy-start(bf16[256,256]{0,1:T(8,128)(2,1)S(1)} %convolution_convert_fusion.2) | copy-start | bytes 393220
  273.8 88.6 %collective-permute-start.12 = (bf16[256,256]{0,1:T(8,128)(2,1)S(1)}, bf16[256,256]{0,1:T(8,128)(2,1)S(1)}, u32[]{:S(2)}, u32[]{:S(2)}) collective-permute-start(bf16[256,256]{0,1:T(8,128)(2,1)S(1)} %get-tuple-element.47), channel_id=1, source_target_pairs={{0,8},{8,16},{16,24},{24,32},{32,40},{40,48},{48,56},{56,64},{64,7... | collective-permute-start | bytes 393224 | tf_op jit(solution)/shard_map/ppermute | solution.py:16
  275.8 86.6 %collective-permute-start.11 = (bf16[256,256]{0,1:T(8,128)(2,1)S(1)}, bf16[256,256]{0,1:T(8,128)(2,1)S(1)}, u32[]{:S(2)}, u32[]{:S(2)}) collective-permute-start(bf16[256,256]{0,1:T(8,128)(2,1)S(1)} %get-tuple-element.47), channel_id=1, source_target_pairs={{0,16},{8,24},{16,32},{24,40},{32,48},{40,56},{48,64},{56,72},{64,... | collective-permute-start | bytes 393224 | tf_op jit(solution)/shard_map/ppermute | solution.py:16
  277.7 84.7 %collective-permute-start.10 = (bf16[256,256]{0,1:T(8,128)(2,1)S(1)}, bf16[256,256]{0,1:T(8,128)(2,1)S(1)}, u32[]{:S(2)}, u32[]{:S(2)}) collective-permute-start(bf16[256,256]{0,1:T(8,128)(2,1)S(1)} %get-tuple-element.47), channel_id=1, source_target_pairs={{0,24},{8,32},{16,40},{24,48},{32,56},{40,64},{48,72},{56,80},{64,... | collective-permute-start | bytes 393224 | tf_op jit(solution)/shard_map/ppermute | solution.py:16
  279.6 32.0 %collective-permute-start.7 = (bf16[256,256]{0,1:T(8,128)(2,1)S(1)}, bf16[256,256]{0,1:T(8,128)(2,1)S(1)}, u32[]{:S(2)}, u32[]{:S(2)}) collective-permute-start(bf16[256,256]{0,1:T(8,128)(2,1)S(1)} %get-tuple-element.47), channel_id=1, source_target_pairs={{0,48},{8,56},{16,64},{24,72},{32,80},{40,88},{48,96},{56,104},{64... | collective-permute-start | bytes 393224 | tf_op jit(solution)/shard_map/ppermute | solution.py:16
  281.8 89.1 %copy-start.21 = (f32[256,128]{0,1:T(8,128)}, f32[256,128]{0,1:T(8,128)S(1)}, u32[]{:S(2)}) copy-start(f32[256,128]{0,1:T(8,128)S(1)} %get-tuple-element.64) | copy-start | bytes 393220
  282.0 89.6 %copy-start.17 = (f32[256,128]{0,1:T(8,128)}, f32[256,128]{0,1:T(8,128)S(1)}, u32[]{:S(2)}) copy-start(f32[256,128]{0,1:T(8,128)S(1)} %get-tuple-element.68) | copy-start | bytes 393220
  282.2 90.0 %copy-start.19 = (f32[256,128]{0,1:T(8,128)}, f32[256,128]{0,1:T(8,128)S(1)}, u32[]{:S(2)}) copy-start(f32[256,128]{0,1:T(8,128)S(1)} %get-tuple-element.72) | copy-start | bytes 393220
  282.4 90.0 %copy-start.15 = (f32[256,128]{0,1:T(8,128)}, f32[256,128]{0,1:T(8,128)S(1)}, u32[]{:S(2)}) copy-start(f32[256,128]{0,1:T(8,128)S(1)} %get-tuple-element.76) | copy-start | bytes 393220
  282.4 27.3 %collective-permute-start.1 = (bf16[256,256]{0,1:T(8,128)(2,1)S(1)}, bf16[256,256]{0,1:T(8,128)(2,1)S(1)}, u32[]{:S(2)}, u32[]{:S(2)}) collective-permute-start(bf16[256,256]{0,1:T(8,128)(2,1)S(1)} %get-tuple-element.48), channel_id=1, source_target_pairs={{0,48},{8,56},{16,64},{24,72},{32,80},{40,88},{48,96},{56,104},{64... | collective-permute-start | bytes 393224 | tf_op jit(solution)/shard_map/ppermute | solution.py:16
  309.7 17.5 %collective-permute-start.2 = (bf16[256,256]{0,1:T(8,128)(2,1)S(1)}, bf16[256,256]{0,1:T(8,128)(2,1)S(1)}, u32[]{:S(2)}, u32[]{:S(2)}) collective-permute-start(bf16[256,256]{0,1:T(8,128)(2,1)S(1)} %get-tuple-element.48), channel_id=1, source_target_pairs={{0,40},{8,48},{16,56},{24,64},{32,72},{40,80},{48,88},{56,96},{64,... | collective-permute-start | bytes 393224 | tf_op jit(solution)/shard_map/ppermute | solution.py:16
  311.7 20.0 %collective-permute-start.3 = (bf16[256,256]{0,1:T(8,128)(2,1)S(1)}, bf16[256,256]{0,1:T(8,128)(2,1)S(1)}, u32[]{:S(2)}, u32[]{:S(2)}) collective-permute-start(bf16[256,256]{0,1:T(8,128)(2,1)S(1)} %get-tuple-element.48), channel_id=1, source_target_pairs={{0,32},{8,40},{16,48},{24,56},{32,64},{40,72},{48,80},{56,88},{64,... | collective-permute-start | bytes 393224 | tf_op jit(solution)/shard_map/ppermute | solution.py:16
  327.2 13.4 %collective-permute-start.4 = (bf16[256,256]{0,1:T(8,128)(2,1)S(1)}, bf16[256,256]{0,1:T(8,128)(2,1)S(1)}, u32[]{:S(2)}, u32[]{:S(2)}) collective-permute-start(bf16[256,256]{0,1:T(8,128)(2,1)S(1)} %get-tuple-element.48), channel_id=1, source_target_pairs={{0,24},{8,32},{16,40},{24,48},{32,56},{40,64},{48,72},{56,80},{64,... | collective-permute-start | bytes 393224 | tf_op jit(solution)/shard_map/ppermute | solution.py:16
  331.7 13.4 %collective-permute-start.5 = (bf16[256,256]{0,1:T(8,128)(2,1)S(1)}, bf16[256,256]{0,1:T(8,128)(2,1)S(1)}, u32[]{:S(2)}, u32[]{:S(2)}) collective-permute-start(bf16[256,256]{0,1:T(8,128)(2,1)S(1)} %get-tuple-element.48), channel_id=1, source_target_pairs={{0,16},{8,24},{16,32},{24,40},{32,48},{40,56},{48,64},{56,72},{64,... | collective-permute-start | bytes 393224 | tf_op jit(solution)/shard_map/ppermute | solution.py:16
  340.6 6.5 collective-permute-start.6
  345.2 13.5 %collective-permute-start.8 = (bf16[256,256]{0,1:T(8,128)(2,1)S(1)}, bf16[256,256]{0,1:T(8,128)(2,1)S(1)}, u32[]{:S(2)}, u32[]{:S(2)}) collective-permute-start(bf16[256,256]{0,1:T(8,128)(2,1)S(1)} %get-tuple-element.47), channel_id=1, source_target_pairs={{0,40},{8,48},{16,56},{24,64},{32,72},{40,80},{48,88},{56,96},{64,... | collective-permute-start | bytes 393224 | tf_op jit(solution)/shard_map/ppermute | solution.py:16
  347.1 15.2 %collective-permute-start.9 = (bf16[256,256]{0,1:T(8,128)(2,1)S(1)}, bf16[256,256]{0,1:T(8,128)(2,1)S(1)}, u32[]{:S(2)}, u32[]{:S(2)}) collective-permute-start(bf16[256,256]{0,1:T(8,128)(2,1)S(1)} %get-tuple-element.47), channel_id=1, source_target_pairs={{0,32},{8,40},{16,48},{24,56},{32,64},{40,72},{48,80},{56,88},{64,... | collective-permute-start | bytes 393224 | tf_op jit(solution)/shard_map/ppermute | solution.py:16
  367.3 4.3 copy-start.28
  368.6 3.6 copy-start.30
  369.4 2.2 copy-start.3
  369.4 3.6 copy-start.32
  371.1 18.3 %copy-start.4 = (bf16[256,128]{0,1:T(8,128)(2,1)}, bf16[256,128]{0,1:T(8,128)(2,1)S(1)}, u32[]{:S(2)}) copy-start(bf16[256,128]{0,1:T(8,128)(2,1)S(1)} %fusion.41) | copy-start | bytes 196612
  371.8 4.7 copy-start.6
  372.4 3.3 copy-start.8
  372.6 2.5 copy-start.10
  377.2 12.6 %collective-permute-start.13 = (bf16[256,256]{0,1:T(8,128)(2,1)S(1)}, bf16[256,256]{0,1:T(8,128)(2,1)S(1)}, u32[]{:S(2)}, u32[]{:S(2)}) collective-permute-start(bf16[256,256]{0,1:T(8,128)(2,1)S(1)} %get-tuple-element.30), channel_id=1, source_target_pairs={{8,0},{16,8},{24,16},{32,24},{40,32},{48,40},{56,48},{64,56},{72,6... | collective-permute-start | bytes 393224 | tf_op jit(solution)/shard_map/ppermute | solution.py:16
  381.6 17.1 %collective-permute-start.18 = (bf16[256,256]{0,1:T(8,128)(2,1)S(1)}, bf16[256,256]{0,1:T(8,128)(2,1)S(1)}, u32[]{:S(2)}, u32[]{:S(2)}) collective-permute-start(bf16[256,256]{0,1:T(8,128)(2,1)S(1)} %get-tuple-element.31), channel_id=1, source_target_pairs={{48,0},{56,8},{64,16},{72,24},{80,32},{88,40},{96,48},{104,56},{11... | collective-permute-start | bytes 393224 | tf_op jit(solution)/shard_map/ppermute | solution.py:16
  383.5 19.1 %collective-permute-start.17 = (bf16[256,256]{0,1:T(8,128)(2,1)S(1)}, bf16[256,256]{0,1:T(8,128)(2,1)S(1)}, u32[]{:S(2)}, u32[]{:S(2)}) collective-permute-start(bf16[256,256]{0,1:T(8,128)(2,1)S(1)} %get-tuple-element.32), channel_id=1, source_target_pairs={{40,0},{48,8},{56,16},{64,24},{72,32},{80,40},{88,48},{96,56},{104... | collective-permute-start | bytes 393224 | tf_op jit(solution)/shard_map/ppermute | solution.py:16
  385.5 23.7 %collective-permute-start.16 = (bf16[256,256]{0,1:T(8,128)(2,1)S(1)}, bf16[256,256]{0,1:T(8,128)(2,1)S(1)}, u32[]{:S(2)}, u32[]{:S(2)}) collective-permute-start(bf16[256,256]{0,1:T(8,128)(2,1)S(1)} %get-tuple-element.33), channel_id=1, source_target_pairs={{32,0},{40,8},{48,16},{56,24},{64,32},{72,40},{80,48},{88,56},{96,... | collective-permute-start | bytes 393224 | tf_op jit(solution)/shard_map/ppermute | solution.py:16
  387.5 31.3 %collective-permute-start.15 = (bf16[256,256]{0,1:T(8,128)(2,1)S(1)}, bf16[256,256]{0,1:T(8,128)(2,1)S(1)}, u32[]{:S(2)}, u32[]{:S(2)}) collective-permute-start(bf16[256,256]{0,1:T(8,128)(2,1)S(1)} %get-tuple-element.34), channel_id=1, source_target_pairs={{24,0},{32,8},{40,16},{48,24},{56,32},{64,40},{72,48},{80,56},{88,... | collective-permute-start | bytes 393224 | tf_op jit(solution)/shard_map/ppermute | solution.py:16
  389.7 31.9 %collective-permute-start.14 = (bf16[256,256]{0,1:T(8,128)(2,1)S(1)}, bf16[256,256]{0,1:T(8,128)(2,1)S(1)}, u32[]{:S(2)}, u32[]{:S(2)}) collective-permute-start(bf16[256,256]{0,1:T(8,128)(2,1)S(1)} %get-tuple-element.35), channel_id=1, source_target_pairs={{16,0},{24,8},{32,16},{40,24},{48,32},{56,40},{64,48},{72,56},{80,... | collective-permute-start | bytes 393224 | tf_op jit(solution)/shard_map/ppermute | solution.py:16
  398.8 43.8 %copy-start.36 = (bf16[3,2048,256]{2,1,0:T(8,128)(2,1)S(1)}, bf16[3,2048,256]{2,1,0:T(8,128)(2,1)}, u32[]{:S(2)}) copy-start(bf16[3,2048,256]{2,1,0:T(8,128)(2,1)} %all-gather.8.cloned.1.call-done) | copy-start | bytes 9437188
  398.8 30.6 %collective-permute-start.19 = (bf16[256,256]{0,1:T(8,128)(2,1)S(1)}, bf16[256,256]{0,1:T(8,128)(2,1)S(1)}, u32[]{:S(2)}, u32[]{:S(2)}) collective-permute-start(bf16[256,256]{0,1:T(8,128)(2,1)S(1)} %get-tuple-element.36), channel_id=1, source_target_pairs={{8,0},{16,8},{24,16},{32,24},{40,32},{48,40},{56,48},{64,56},{72,6... | collective-permute-start | bytes 393224 | tf_op jit(solution)/shard_map/ppermute | solution.py:16
  402.7 29.5 %collective-permute-start.24 = (bf16[256,256]{0,1:T(8,128)(2,1)S(1)}, bf16[256,256]{0,1:T(8,128)(2,1)S(1)}, u32[]{:S(2)}, u32[]{:S(2)}) collective-permute-start(bf16[256,256]{0,1:T(8,128)(2,1)S(1)} %get-tuple-element.37), channel_id=1, source_target_pairs={{48,0},{56,8},{64,16},{72,24},{80,32},{88,40},{96,48},{104,56},{11... | collective-permute-start | bytes 393224 | tf_op jit(solution)/shard_map/ppermute | solution.py:16
  409.3 25.3 %collective-permute-start.23 = (bf16[256,256]{0,1:T(8,128)(2,1)S(1)}, bf16[256,256]{0,1:T(8,128)(2,1)S(1)}, u32[]{:S(2)}, u32[]{:S(2)}) collective-permute-start(bf16[256,256]{0,1:T(8,128)(2,1)S(1)} %get-tuple-element.38), channel_id=1, source_target_pairs={{40,0},{48,8},{56,16},{64,24},{72,32},{80,40},{88,48},{96,56},{104... | collective-permute-start | bytes 393224 | tf_op jit(solution)/shard_map/ppermute | solution.py:16
  418.7 18.8 %collective-permute-start.22 = (bf16[256,256]{0,1:T(8,128)(2,1)S(1)}, bf16[256,256]{0,1:T(8,128)(2,1)S(1)}, u32[]{:S(2)}, u32[]{:S(2)}) collective-permute-start(bf16[256,256]{0,1:T(8,128)(2,1)S(1)} %get-tuple-element.39), channel_id=1, source_target_pairs={{32,0},{40,8},{48,16},{56,24},{64,32},{72,40},{80,48},{88,56},{96,... | collective-permute-start | bytes 393224 | tf_op jit(solution)/shard_map/ppermute | solution.py:16
  421.6 17.8 %collective-permute-start.21 = (bf16[256,256]{0,1:T(8,128)(2,1)S(1)}, bf16[256,256]{0,1:T(8,128)(2,1)S(1)}, u32[]{:S(2)}, u32[]{:S(2)}) collective-permute-start(bf16[256,256]{0,1:T(8,128)(2,1)S(1)} %get-tuple-element.40), channel_id=1, source_target_pairs={{24,0},{32,8},{40,16},{48,24},{56,32},{64,40},{72,48},{80,56},{88,... | collective-permute-start | bytes 393224 | tf_op jit(solution)/shard_map/ppermute | solution.py:16
  429.4 13.0 %collective-permute-start.20 = (bf16[256,256]{0,1:T(8,128)(2,1)S(1)}, bf16[256,256]{0,1:T(8,128)(2,1)S(1)}, u32[]{:S(2)}, u32[]{:S(2)}) collective-permute-start(bf16[256,256]{0,1:T(8,128)(2,1)S(1)} %get-tuple-element.41), channel_id=1, source_target_pairs={{16,0},{24,8},{32,16},{40,24},{48,32},{56,40},{64,48},{72,56},{80,... | collective-permute-start | bytes 393224 | tf_op jit(solution)/shard_map/ppermute | solution.py:16
  442.5 2.4 copy-start.2
  444.6 333.0 %reduce-scatter.6.cloned.1.call-start = ((), (), s32[]{:S(2)}) async-start(), calls=%async_computation.5 | async-start | bytes 1179648 | tf_op jit(solution)/shard_map/reduce_scatter | solution.py:135
  447.2 330.4 %reduce-scatter.10.cloned.1.call-start = ((), (), s32[]{:S(2)}) async-start(), calls=%async_computation.8 | async-start | bytes 2129920
  460.8 1.2 copy-start.18
  460.8 1.2 copy-start.29
  460.8 1.4 copy-start.20
  460.8 1.4 copy-start.31
  460.8 1.5 copy-start.16
  460.8 1.5 copy-start.33
  462.0 1.3 copy-start.5
  762.8 13.1 %collective-permute-start.25 = (bf16[3,256]{1,0:T(4,128)(2,1)S(1)}, bf16[3,256]{1,0:T(4,128)(2,1)S(1)}, u32[]{:S(2)}, u32[]{:S(2)}) collective-permute-start(bf16[3,256]{1,0:T(4,128)(2,1)S(1)} %slice.288), channel_id=1, source_target_pairs={{8,0},{16,8},{24,16},{32,24},{40,32},{48,40},{56,48},{64,56},{72,6... | collective-permute-start | bytes 4616 | tf_op jit(solution)/shard_map/ppermute | solution.py:16
  (5 other events, 5.1 us)
Sparse Core Ops, SparseCore 0:
  20.4 43.6 all-gather.11
  67.4 87.0 all-gather.9
  157.8 81.0 all-gather.7
  444.7 45.6 reduce-scatter.7
  493.7 44.5 reduce-scatter.5
  543.3 148.3 reduce-scatter.9
where the time goes:
time: 786 us; the launch traced here: 784 us
  blocking collectives  539 us (69%)
  starting transfers between devices  85.1 us (11%)
  waiting for transfers between devices  83.6 us (11%)
  matrix products  30.3 us (4%)
  between operations  29.6 us (4%)
  other arithmetic  10.1 us (1%)
    psum x1, blocking collectives, shards(): lax.psum((jnp.concatenate(grads_tk, 1), jnp.concatenate(grads_tv, 1)), 's...  277 us
    ppermute x26, starting transfers between devices, from_behind(): return lax.ppermute(block, axis, route)  84.7 us
    all_gather x1, blocking collectives, shards(): lax.all_gather(text_states, 'seq', axis=0, tiled=True)  83.4 us
    ppermute x26, waiting for transfers between devices, from_behind(): return lax.ppermute(block, axis, route)  82.7 us
    all_gather x1, blocking collectives, shards(): lax.all_gather(w_text_value, 'seq', axis=0, tiled=True)  80.5 us
    all_gather x1, blocking collectives, shards(): lax.all_gather(w_text_key, 'seq', axis=0, tiled=True)  78.5 us
    psum x1, blocking collectives, shards(): lax.psum((jnp.sum(scaled, 1), jnp.sum(scaled * unit_local, 1)), 'tensor')  19.4 us
  transfers between devices with their start and end apart: 32, of which 14 were waited for; matrix products, arithmetic and copies ran while one was open for 3% of the time, Pallas kernels for 0%

commit v1 on v0

v1 whole, which is shorter than its diff:
```python
import functools

import jax
import jax.numpy as jnp
from jax import lax
from jax.experimental import pallas as pl
from jax.experimental.pallas import tpu as pltpu
from jax.sharding import PartitionSpec as P

HD = 64
WINDOW = 1500
EPS = 1e-05
RING = 8
MESH = pl.DeviceIdType.MESH
BF = jnp.bfloat16
F32 = jnp.float32


def dims_of(n_seq):
    z = min(RING, n_seq // 2)
    return n_seq // (2 * z), z


def nt(a, b):
    return lax.dot_general(a, b, (((1,), (1,)), ((), ())), preferred_element_type=F32)


def nn(a, b):
    return lax.dot_general(a, b, (((1,), (0,)), ((), ())), preferred_element_type=F32)


def tn(a, b):
    return lax.dot_general(a, b, (((0,), (0,)), ((), ())), preferred_element_type=F32)


def send(src, dst, ssem, rsem, seq, ten):
    return pltpu.make_async_remote_copy(
        src_ref=src, dst_ref=dst, send_sem=ssem, recv_sem=rsem, device_id=(seq, ten), device_id_type=MESH
    )


def greet(partners):
    sem = pltpu.get_barrier_semaphore()
    for seq, ten in partners:
        pl.semaphore_signal(sem, inc=1, device_id=(seq, ten), device_id_type=MESH)
    pl.semaphore_wait(sem, len(partners))


class Place:
    def __init__(self, n_seq, n_ten):
        self.n_seq, self.n_ten = n_seq, n_ten
        self.H, self.Z = dims_of(n_seq)
        self.s = lax.axis_index("seq")
        self.t = lax.axis_index("tensor")
        self.c = lax.rem(self.s, 2)
        self.p = lax.div(self.s, 2)
        self.h = lax.div(self.p, self.Z)
        self.z = lax.rem(self.p, self.Z)
        self.chips = n_seq // 2

    def seq(self, h, z, c):
        return (h * self.Z + z) * 2 + c

    def sibling(self):
        return self.seq(self.h, self.z, 1 - self.c)

    def chip(self, k):
        return lax.rem(self.p + k + self.chips, self.chips) * 2 + self.c

    def other_h(self, d):
        return lax.rem(self.h + d, self.H)

    def other_z(self, d):
        return lax.rem(self.z + d + self.Z, self.Z)

    def other_t(self, d):
        return lax.rem(self.t + d + self.n_ten, self.n_ten)

    def next(self, d):
        return lax.rem(self.s + d + self.n_seq, self.n_seq)


def gather_kernel(
    n_seq, n_ten, pay, loc, head, rim, cot, g, f, cotx,
    rimbuf, blk, lsem, one_s, one_r, h_s, h_r, z_s, z_r, f_s, f_r, x_s, x_r,
):
    me = Place(n_seq, n_ten)
    H, Z, T = me.H, me.Z, n_ten
    s, t, c, h, z = me.s, me.t, me.c, me.h, me.z
    sib = me.sibling()
    half = Z // 2
    width = loc.shape[1]
    partners = [(sib, t), (me.next(1), t), (me.next(-1), t)]
    partners += [(me.seq(me.other_h(d), z, c), t) for d in range(1, H)]
    right, left = me.seq(h, me.other_z(1), c), me.seq(h, me.other_z(-1), c)
    partners += [(right, t), (left, t)]
    partners += [(s, me.other_t(d)) for d in range(1, T)]
    greet(partners)

    outgoing = []

    def go(copy):
        copy.start()
        outgoing.append(copy)

    def cols(ref, core, ten):
        return ref.at[core, :, pl.ds(pl.multiple_of(ten * width, width), width)]

    go(send(pay.at[1 - c], g.at[h, z, c], one_s.at[0], one_r.at[0], sib, t))
    go(send(rim, rimbuf, one_s.at[1], one_r.at[1], me.next(1), t))
    mine = pltpu.make_async_copy(pay.at[c], g.at[h, z, c], lsem.at[0])
    mine.start()
    blk[...] = loc[...]
    send(rim, rimbuf, one_s.at[1], one_r.at[1], me.next(1), t).wait_recv()
    blk[0:16, :] = (head[...] + jnp.where(s > 0, rimbuf[...], 0.0)).astype(BF)
    for d in range(1, T):
        go(send(blk, cols(f, c, t), f_s.at[d], f_r.at[d], s, me.other_t(d)))
    go(send(blk, cols(f, c, t), x_s.at[0], x_r.at[0], sib, t))
    own = pltpu.make_async_copy(blk, cols(f, c, t), lsem.at[1])
    own.start()
    mine.wait()
    send(pay.at[c], g.at[h, z, 1 - c], one_s.at[0], one_r.at[0], sib, t).wait_recv()
    for d in range(1, H):
        go(send(g.at[h, z], g.at[h, z], h_s.at[d], h_r.at[d], me.seq(me.other_h(d), z, c), t))

    def step(way, k, d, first):
        hh = me.other_h(d)
        zz = me.other_z(-(k - 1) if way == 0 else k - 1)
        go(send(g.at[hh, zz], g.at[hh, zz], z_s.at[way, k, d], z_r.at[way, k, d], right if way == 0 else left, t))

    def arrived(way, k, d):
        hh = me.other_h(d)
        zz = me.other_z(-k if way == 0 else k)
        send(g.at[hh, zz], g.at[hh, zz], z_s.at[way, k, d], z_r.at[way, k, d], right, t).wait_recv()

    def used(way, k, d):
        if k < half:
            return True
        if k > half:
            return False
        return (d < H // 2) if way == 0 else (d >= H // 2)

    for d in range(H):
        if d:
            hh = me.other_h(H - d)
            send(g.at[hh, z], g.at[hh, z], h_s.at[d], h_r.at[d], sib, t).wait_recv()
        dd = (H - d) % H
        for way in (0, 1):
            if used(way, 1, dd):
                step(way, 1, dd, True)
    go(send(cot, cotx, one_s.at[2], one_r.at[2], sib, t))
    for k in range(1, half + 1):
        if k == max(half - 1, 1):
            for d in range(1, T):
                tt = me.other_t(-d)
                send(blk, cols(f, c, tt), f_s.at[d], f_r.at[d], sib, t).wait_recv()
                go(send(cols(f, c, tt), cols(f, c, tt), x_s.at[d], x_r.at[d], sib, t))
        for d in [0] + [(H - e) % H for e in range(1, H)]:
            for way in (0, 1):
                if used(way, k, d):
                    arrived(way, k, d)
                    if used(way, k + 1, d):
                        step(way, k + 1, d, False)
    own.wait()
    for d in range(T):
        tt = me.other_t(-d)
        send(blk, cols(f, 1 - c, tt), x_s.at[d], x_r.at[d], sib, t).wait_recv()
    send(cot, cotx, one_s.at[2], one_r.at[2], sib, t).wait_recv()
    for copy in outgoing:
        copy.wait_send()


def gather(n_seq, n_ten, pay, loc, head, rim, cot):
    H, Z = dims_of(n_seq)
    frames, width = loc.shape
    dma = pltpu.SemaphoreType.DMA
    vm = pl.BlockSpec(memory_space=pltpu.VMEM)
    anywhere = pl.BlockSpec(memory_space=pl.ANY)
    return pl.pallas_call(
        functools.partial(gather_kernel, n_seq, n_ten),
        out_shape=(
            jax.ShapeDtypeStruct((H, Z) + pay.shape, BF),
            jax.ShapeDtypeStruct((2, frames, width * n_ten), BF),
            jax.ShapeDtypeStruct(cot.shape, BF),
        ),
        in_specs=[vm, vm, vm, vm, anywhere],
        out_specs=(anywhere, anywhere, anywhere),
        scratch_shapes=[
            pltpu.VMEM(rim.shape, F32),
            pltpu.VMEM(loc.shape, BF),
            dma((2,)),
            dma((3,)), dma((3,)),
            dma((H,)), dma((H,)),
            dma((2, Z // 2 + 1, H)), dma((2, Z // 2 + 1, H)),
            dma((n_ten,)), dma((n_ten,)),
            dma((n_ten,)), dma((n_ten,)),
        ],
        compiler_params=pltpu.CompilerParams(collective_id=0, has_side_effects=True, vmem_limit_bytes=16 << 20),
    )(pay, loc, head, rim, cot)


def attention_kernel(
    n_seq, n_ten, kv, qd, tkv, tmask, att, dq, dk, dv, tkg, tvg,
    kx, qx, wbuf, wtbuf, st, cstat, lsem, k_s, k_r, q_s, q_r, t_s, t_r,
):
    me = Place(n_seq, n_ten)
    t, p = me.t, me.p
    B = kv.shape[0]
    q_rows = B // 2
    greet([(me.chip(k), t) for k in (1, -1, 2, -2, 3, -3)])
    outgoing = []

    def go(copy):
        copy.start()
        outgoing.append(copy)

    def kslot(k):
        return kx.at[pl.ds((3 - k) * B, B)]

    def qslot(k):
        return qx.at[pl.ds(k * B, B)]

    go(send(kv, kslot(1), k_s.at[0], k_r.at[0], me.chip(1), t))
    go(send(qd, qslot(1), q_s.at[0], q_r.at[0], me.chip(-1), t))
    a = pltpu.make_async_copy(kv, kslot(0), lsem.at[0])
    b = pltpu.make_async_copy(qd, qslot(0), lsem.at[1])
    a.start()
    b.start()
    a.wait()
    b.wait()
    for k in (1, 2, 3):
        send(kv, kslot(k), k_s.at[k - 1], k_r.at[k - 1], me.chip(1), t).wait_recv()
        if k < 3:
            go(send(kslot(k), kslot(k + 1), k_s.at[k], k_r.at[k], me.chip(1), t))
        send(qd, qslot(k), q_s.at[k - 1], q_r.at[k - 1], me.chip(-1), t).wait_recv()
        if k < 3:
            go(send(qslot(k), qslot(k + 1), q_s.at[k], q_r.at[k], me.chip(-1), t))

    lane = lax.broadcasted_iota(jnp.int32, (q_rows, 128), 1)
    row = lax.broadcasted_iota(jnp.int32, (q_rows, q_rows), 0)
    col = lax.broadcasted_iota(jnp.int32, (q_rows, q_rows), 1)
    heads = [lane < HD, lane >= HD]
    chunks = (WINDOW + q_rows - 2) // q_rows + 1
    lead = (chunks - 1) * q_rows
    scale = HD ** (-0.5)
    zero = jnp.zeros((), BF)
    live = tmask[0:1, :] > 0.0

    def forward(qb, carry):
        rows = pl.ds(pl.multiple_of(qb * q_rows, q_rows), q_rows)
        q_both = qx[rows, 0:128]
        d_both = qx[rows, 128:256]
        parts = []
        stats = []
        for hd in range(2):
            q = jnp.where(heads[hd], q_both, zero) * jnp.asarray(scale, BF)
            wt = jnp.where(live, jnp.exp(nt(q, tkv[:, 0:128])), 0.0)
            wtbuf[qb, hd] = wt
            total = wt
            mix = nn(wt.astype(BF), tkv[:, 128:256])
            for j in range(chunks):
                base = pl.multiple_of((qb + j) * q_rows, q_rows)
                w = jnp.exp(nt(q, kx[pl.ds(base, q_rows), 0:128]))
                ok = p * B - 3 * B + (qb + j) * q_rows >= 0
                if j * q_rows - lead + q_rows + WINDOW - 1 < q_rows + q_rows - 1:
                    ok = ok & (lead + row - j * q_rows - col < WINDOW)
                if j == chunks - 1:
                    ok = ok & (col <= row)
                w = jnp.where(ok, w, 0.0)
                wbuf[qb, hd, j] = w
                total = total + w[:, 0:128] + w[:, 128:256]
                mix = mix + nn(w.astype(BF), kx[pl.ds(base, q_rows), 128:256])
            total = jnp.sum(total, 1, keepdims=True)
            a_head = (mix / total).astype(BF)
            parts.append(a_head)
            inner = jnp.sum(
                jnp.where(heads[hd], d_both.astype(F32) * a_head.astype(F32), 0.0), 1, keepdims=True
            )
            stats.append((1.0 / total, inner))
        att[rows, :] = jnp.where(heads[0], parts[0], parts[1])
        (r0, i0), (r1, i1) = stats
        packed = jnp.where(lane == 0, r0, jnp.where(lane == 1, r1, jnp.where(lane == 2, i0, i1)))
        cstat[rows, :] = packed
        st[0, :, pl.ds(pl.multiple_of(qb * q_rows, q_rows), q_rows)] = packed.T[0:8, :]
        return carry

    lax.fori_loop(0, 2, forward, 0)
    for k in (1, 2, 3):
        go(send(st.at[0], st.at[k], t_s.at[k], t_r.at[k], me.chip(-k), t))

    tkg[...] = jnp.zeros_like(tkg)
    tvg[...] = jnp.zeros_like(tvg)

    def query_grads(qb, carry):
        rows = pl.ds(pl.multiple_of(qb * q_rows, q_rows), q_rows)
        q_both = qx[rows, 0:128]
        d_both = qx[rows, 128:256]
        parts = []
        for hd in range(2):
            q = jnp.where(heads[hd], q_both, zero)
            d = jnp.where(heads[hd], d_both, zero)
            r = cstat[rows, hd : hd + 1]
            inner = cstat[rows, 2 + hd : 3 + hd]
            sh = wtbuf[qb, hd] * r
            ds = (sh * (nt(d, tkv[:, 128:256]) - inner)).astype(BF)
            grad = nn(ds, tkv[:, 0:128])
            tkg[...] += tn(ds, q) * scale
            tvg[...] += tn(sh.astype(BF), d)
            for j in range(chunks):
                base = pl.multiple_of((qb + j) * q_rows, q_rows)
                keys = kx[pl.ds(base, q_rows), :]
                ds = (wbuf[qb, hd, j] * r * (nt(d, keys[:, 128:256]) - inner)).astype(BF)
                grad = grad + nn(ds, keys[:, 0:128])
            parts.append(grad)
        dq[rows, :] = (jnp.where(heads[0], parts[0], parts[1]) * scale).astype(BF)
        return carry

    lax.fori_loop(0, 2, query_grads, 0)
    for k in (1, 2, 3):
        send(st.at[0], st.at[k], t_s.at[k], t_r.at[k], me.chip(-k), t).wait_recv()

    def key_grads(kb, carry):
        rows = pl.ds(pl.multiple_of(kb * q_rows, q_rows), q_rows)
        k_both = kv[rows, 0:128]
        v_both = kv[rows, 128:256]
        kparts, vparts = [], []
        for hd in range(2):
            kh = jnp.where(heads[hd], k_both, zero) * jnp.asarray(scale, BF)
            vh = jnp.where(heads[hd], v_both, zero)
            gk = jnp.zeros((q_rows, 128), F32)
            gv = jnp.zeros((q_rows, 128), F32)
            for i in range(chunks):
                base = pl.multiple_of((kb + i) * q_rows, q_rows)
                qs = qx[pl.ds(base, q_rows), :]
                blk = lax.div(kb + i, 2)
                part = pl.ds(pl.multiple_of(lax.rem(kb + i, 2) * q_rows, q_rows), q_rows)
                r = st[blk, hd : hd + 1, part]
                inner = st[blk, 2 + hd : 3 + hd, part]
                ok = p * B + (kb + i) * q_rows < n_seq * q_rows
                if i == 0:
                    ok = ok & (col >= row)
                if i * q_rows + q_rows - 1 >= WINDOW:
                    ok = ok & (i * q_rows + col - row < WINDOW)
                sh = jnp.where(ok, jnp.exp(nt(kh, qs[:, 0:128])) * r, 0.0)
                ds = (sh * (nt(vh, qs[:, 128:256]) - inner)).astype(BF)
                gv = gv + nn(sh.astype(BF), qs[:, 128:256])
                gk = gk + nn(ds, qs[:, 0:128])
            kparts.append(gk)
            vparts.append(gv)
        dk[rows, :] = (jnp.where(heads[0], kparts[0], kparts[1]) * scale).astype(BF)
        dv[rows, :] = jnp.where(heads[0], vparts[0], vparts[1]).astype(BF)
        return carry

    lax.fori_loop(0, 2, key_grads, 0)
    for copy in outgoing:
        copy.wait_send()


def attention(n_seq, n_ten, kv, qd, tkv, tmask):
    B = kv.shape[0]
    Q = B // 2
    text = tkv.shape[0]
    chunks = (WINDOW + Q - 2) // Q + 1
    dma = pltpu.SemaphoreType.DMA
    vm = pl.BlockSpec(memory_space=pltpu.VMEM)
    rows = jax.ShapeDtypeStruct((B, 128), BF)
    small = jax.ShapeDtypeStruct((text, 128), F32)
    return pl.pallas_call(
        functools.partial(attention_kernel, n_seq, n_ten),
        out_shape=(rows, rows, rows, rows, small, small),
        in_specs=[vm] * 4,
        out_specs=(vm,) * 6,
        scratch_shapes=[
            pltpu.VMEM((4 * B, 256), BF),
            pltpu.VMEM((4 * B, 256), BF),
            pltpu.VMEM((2, 2, chunks, Q, Q), F32),
            pltpu.VMEM((2, 2, Q, text), F32),
            pltpu.VMEM((4, 8, B), F32),
            pltpu.VMEM((B, 128), F32),
            dma((2,)),
            dma((3,)), dma((3,)),
            dma((3,)), dma((3,)),
            dma((4,)), dma((4,)),
        ],
        compiler_params=pltpu.CompilerParams(collective_id=1, has_side_effects=True, vmem_limit_bytes=40 << 20),
    )(kv, qd, tkv, tmask)


def scatter_kernel(
    n_seq, n_ten, op, ip, sg, ns, unit, inv, gain, out, fg, rim, sgo,
    opx, ipx, nsx, ops, ips, nss, opr, ipr, nsr, sgz, sgh, sghr, sgs, sgx,
    x_s, x_r, z_s, z_r, h_s, h_r, o_s, o_r, i_s, i_r, n_s, n_r, l_s, l_r,
):
    me = Place(n_seq, n_ten)
    H, Z, T = me.H, me.Z, n_ten
    s, t, c, h, z = me.s, me.t, me.c, me.h, me.z
    sib = me.sibling()
    width = out.shape[1]
    partners = [(sib, t), (me.next(1), t), (me.next(-1), t)]
    partners += [(me.seq(me.other_h(d), z, c), t) for d in range(1, H)]
    partners += [(me.seq(h, me.other_z(d), c), t) for d in range(1, Z)]
    partners += [(s, me.other_t(d)) for d in range(1, T)]
    greet(partners)
    outgoing = []

    def go(copy):
        copy.start()
        outgoing.append(copy)

    def cols(ref, ten):
        return ref.at[:, pl.ds(pl.multiple_of(ten * width, width), width)]

    def window(ten):
        return pl.ds(pl.multiple_of(ten * width, width), width)

    for d in range(T):
        tt = me.other_t(d)
        go(send(cols(ip.at[1 - c], tt), cols(ipx, tt), x_s.at[0, d], x_r.at[0, d], sib, t))
    go(send(ns.at[1 - c], nsx, l_s.at[0], l_r.at[0], sib, t))
    for d in range(1, Z):
        zz = me.other_z(d)
        go(send(sg.at[zz], sgz.at[d], z_s.at[d], z_r.at[d], me.seq(h, zz, c), t))
    for d in range(T):
        tt = me.other_t(d)
        go(send(cols(op.at[1 - c], tt), cols(opx, tt), x_s.at[1, d], x_r.at[1, d], sib, t))

    def exchange(which, own, from_sib, summed, landing, ss, rr):
        for d in [*range(1, T), 0]:
            tt = me.other_t(d)
            send(cols(from_sib, tt), cols(from_sib, tt), x_s.at[which, d], x_r.at[which, d], sib, t).wait_recv()
            both = own[c, :, window(tt)].astype(F32) + from_sib[:, window(tt)].astype(F32)
            summed[d] = both.astype(BF)
            if d:
                go(send(summed.at[d], landing.at[d], ss.at[d], rr.at[d], s, tt))

    exchange(0, ip, ipx, ips, ipr, i_s, i_r)
    send(nsx, nsx, l_s.at[0], l_r.at[0], sib, t).wait_recv()
    nss[...] = ns[c] + nsx[...]
    for d in range(1, T):
        go(send(nss, nsr.at[d], n_s.at[d], n_r.at[d], s, me.other_t(d)))
    exchange(1, op, opx, ops, opr, o_s, o_r)
    acc = sg[z].astype(F32)
    for d in range(1, Z):
        send(sg.at[0], sgz.at[d], z_s.at[d], z_r.at[d], sib, t).wait_recv()
        acc = acc + sgz[d].astype(F32)
    sgh[...] = acc
    for d in range(1, H):
        hh = me.other_h(d)
        go(send(sgh.at[hh], sghr.at[d], h_s.at[d], h_r.at[d], me.seq(hh, z, c), t))
    total = ips[0].astype(F32)
    sums = nss[...]
    for d in range(1, T):
        send(ips.at[d], ipr.at[d], i_s.at[d], i_r.at[d], sib, t).wait_recv()
        total = total + ipr[d].astype(F32)
        send(nss, nsr.at[d], n_s.at[d], n_r.at[d], sib, t).wait_recv()
        sums = sums + nsr[d]
    full = width * T
    tall = jnp.concatenate([sums] * (128 // sums.shape[0]), 0).T
    mean_plain = tall[:, 0:1] / full
    mean_unit = tall[:, 1:2] / full
    grad = inv[:, 0:1] * (total * gain[0:1, :] - mean_plain - unit[...] * mean_unit)
    fg[...] = grad.astype(BF)
    go(send(fg.at[pl.ds(0, 16)], rim, l_s.at[1], l_r.at[1], me.next(-1), t))
    acc = sgh[h]
    for d in range(1, H):
        send(sgh.at[0], sghr.at[d], h_s.at[d], h_r.at[d], sib, t).wait_recv()
        acc = acc + sghr[d]
    sgs[...] = acc
    go(send(sgs.at[1 - c], sgx, l_s.at[2], l_r.at[2], sib, t))
    total = ops[0].astype(F32)
    for d in range(1, T):
        send(ops.at[d], opr.at[d], o_s.at[d], o_r.at[d], sib, t).wait_recv()
        total = total + opr[d].astype(F32)
    out[...] = total.astype(BF)
    send(sgs.at[0], sgx, l_s.at[2], l_r.at[2], sib, t).wait_recv()
    sgo[:, 0:128] = jnp.where(c == 0, sgs[c], sgx[...])
    sgo[:, 128:256] = jnp.where(c == 0, sgx[...], sgs[c])
    send(rim, rim, l_s.at[1], l_r.at[1], sib, t).wait_recv()
    for copy in outgoing:
        copy.wait_send()


def scatter(n_seq, n_ten, op, ip, sg, ns, unit, inv, gain):
    H, Z = dims_of(n_seq)
    T = n_ten
    frames, width = unit.shape
    rows = sg.shape[3]
    dma = pltpu.SemaphoreType.DMA
    vm = pl.BlockSpec(memory_space=pltpu.VMEM)
    block = pltpu.VMEM((T, frames, width), BF)
    return pl.pallas_call(
        functools.partial(scatter_kernel, n_seq, n_ten),
        out_shape=(
            jax.ShapeDtypeStruct((frames, width), BF),
            jax.ShapeDtypeStruct((frames, width), BF),
            jax.ShapeDtypeStruct((16, width), BF),
            jax.ShapeDtypeStruct((rows, 256), F32),
        ),
        in_specs=[vm] * 7,
        out_specs=(vm,) * 4,
        scratch_shapes=[
            pltpu.VMEM(op.shape[1:], BF),
            pltpu.VMEM(ip.shape[1:], BF),
            pltpu.VMEM(ns.shape[1:], F32),
            block, block,
            pltpu.VMEM(ns.shape[1:], F32),
            block, block,
            pltpu.VMEM((T,) + ns.shape[1:], F32),
            pltpu.VMEM(sg.shape, BF),
            pltpu.VMEM(sg.shape[1:], F32),
            pltpu.VMEM(sg.shape[1:], F32),
            pltpu.VMEM(sg.shape[2:], F32),
            pltpu.VMEM(sg.shape[3:], F32),
            dma((2, T)), dma((2, T)),
            dma((Z,)), dma((Z,)),
            dma((H,)), dma((H,)),
            dma((T,)), dma((T,)),
            dma((T,)), dma((T,)),
            dma((T,)), dma((T,)),
            dma((3,)), dma((3,)),
        ],
        compiler_params=pltpu.CompilerParams(collective_id=2, has_side_effects=True, vmem_limit_bytes=40 << 20),
    )(op, ip, sg, ns, unit, inv, gain)


def shards(
    n_seq, n_ten, embedded, delays, norm_gain, w_query, w_key, w_value, w_out,
    text_states, w_text_key, w_text_value, text_len, cotangent,
):
    H, Z = dims_of(n_seq)
    frames, books, width = embedded.shape
    full = width * n_ten
    seq = lax.axis_index("seq")
    core = lax.rem(seq, 2)
    ten = lax.axis_index("tensor")
    R = w_query.shape[0]
    tr = w_text_key.shape[0]
    text = text_states.shape[0] * n_seq
    tdim = text_states.shape[1]

    longer = jnp.zeros((frames + 16, width), F32)
    for d in range(books):
        book = jnp.zeros((frames, width), F32)
        for k in range(books):
            book = book + jnp.where(delays[k] == d, embedded[:, k].astype(F32), 0.0)
        longer = longer + jnp.pad(book, ((d, 16 - d), (0, 0)))
    local = longer[:frames]
    rim = longer[frames:]

    states_flat = text_states.reshape(-1)
    states_flat = jnp.pad(states_flat, (0, 2048 - states_flat.shape[0])).reshape(16, 128)
    pieces = [w_query, w_key, w_value, w_out.T]
    pieces += [jnp.pad(w, ((0, 16 - tr), (0, 0))) for w in (w_text_key, w_text_value)]
    pay = jnp.concatenate(pieces, 0)
    pay = jnp.stack(
        [jnp.concatenate([pay[:, i * 128 : (i + 1) * 128], states_flat], 0) for i in range(2)], 0
    )
    g, f, cotx = gather(n_seq, n_ten, pay, local.astype(BF), local[:16], rim, cotangent)

    def part(a, n):
        return g[:, :, :, a : a + n, :].reshape(-1, 128)

    wq, wk, wv, wo = (part(i * R, R) for i in range(4))
    wtk, wtv = part(4 * R, tr), part(4 * R + 16, tr)
    states = g[:, :, :, 4 * R + 32 : 4 * R + 48, :].reshape(n_seq, 2048)
    states = states[:, : text_states.size].reshape(text, tdim)

    x = f.reshape(2 * frames, full).astype(F32)
    mean = jnp.mean(x, -1, keepdims=True)
    centred = x - mean
    inv_std = lax.rsqrt(jnp.mean(centred * centred, -1, keepdims=True) + EPS)
    unit = centred * inv_std
    normed = (unit * norm_gain).astype(BF)
    cot = jnp.where(core == 0, jnp.stack([cotangent, cotx]), jnp.stack([cotx, cotangent]))
    cot = cot.reshape(2 * frames, full)
    kv = jnp.concatenate([nn(normed, wk).astype(BF), nn(normed, wv).astype(BF)], 1)
    qd = jnp.concatenate([nn(normed, wq).astype(BF), nn(cot, wo).astype(BF)], 1)
    tkv = jnp.concatenate([nn(states, wtk).astype(BF), nn(states, wtv).astype(BF)], 1)
    tmask = (lax.broadcasted_iota(jnp.int32, (8, text), 1) < text_len[0]).astype(F32)

    att, dq, dk, dv, tkg, tvg = attention(n_seq, n_ten, kv, qd, tkv, tmask)

    op = nt(att, wo).astype(BF).reshape(2, frames, full)
    ipf = nt(dq, wq) + nt(dk, wk) + nt(dv, wv)
    scaled = ipf * norm_gain
    ns = jnp.stack([jnp.sum(scaled, 1), jnp.sum(scaled * unit, 1)], 0).reshape(2, 2, frames)
    ns = jnp.pad(ns.transpose(1, 0, 2), ((0, 0), (0, 6), (0, 0)))
    ip = ipf.astype(BF).reshape(2, frames, full)

    def by_owner(grads, rows, padded):
        grads = grads.reshape(H, Z, 2, rows, 128)
        grads = jnp.pad(grads, ((0, 0), (0, 0), (0, 0), (0, padded - rows), (0, 0)))
        return grads.transpose(1, 0, 2, 3, 4)

    sg = jnp.concatenate(
        [
            by_owner(tn(cot, att), R, R),
            by_owner(tn(states, tkg.astype(BF)), tr, 16),
            by_owner(tn(states, tvg.astype(BF)), tr, 16),
        ],
        3,
    ).astype(BF)
    unit_here = lax.dynamic_slice(unit, (core * frames, ten * width), (frames, width))
    inv_here = jnp.broadcast_to(lax.dynamic_slice_in_dim(inv_std, core * frames, frames, 0), (frames, 128))
    gain_here = jnp.broadcast_to(lax.dynamic_slice_in_dim(norm_gain, ten * width, width, 0)[None], (8, width))
    out, fg, above, sgo = scatter(n_seq, n_ten, op, ip, sg, ns, unit_here, inv_here, gain_here)
    above = jnp.where(seq < n_seq - 1, above, jnp.zeros_like(above))
    longer = jnp.concatenate([fg, above], 0)
    d_embedded = jnp.stack(
        [
            functools.reduce(
                lambda x, d: jnp.where(delays[k] == d, longer[d : d + frames], x),
                range(1, books),
                longer[:frames],
            )
            for k in range(books)
        ],
        1,
    )
    return (out, d_embedded, sgo[:R].T, sgo[R : R + tr], sgo[R + 16 : R + 16 + tr])


def solution(mesh):
    placed = (
        P("seq", None, "tensor"), P(), P(),
        P("seq", "tensor"), P("seq", "tensor"), P("seq", "tensor"), P("tensor", "seq"),
        P("seq", None), P("seq", "tensor"), P("seq", "tensor"), P(), P("seq", None),
    )
    return jax.shard_map(
        functools.partial(shards, mesh.shape["seq"], mesh.shape["tensor"]),
        mesh=mesh,
        in_specs=placed,
        out_specs=(
            P("seq", "tensor"), P("seq", None, "tensor"), P("tensor", "seq"),
            P("seq", "tensor"), P("seq", "tensor"),
        ),
        check_vma=False,
    )
```

time: 786 us -> 215 us (0.27)
  the two profiles are of different devices: /device:TPU:33 before, /device:TPU:1 now
where the time goes in v1:
time: 215 us; the launch traced here: 214 us
  Pallas kernels  159 us (74%)
  local copies, waits for them, and re-layouts  24.3 us (11%)
  matrix products  12.7 us (6%)
  between operations  12.4 us (6%)
  other arithmetic  5.51 us (3%)
    pallas_call x1, Pallas kernels, gather(): pl.pallas_call(functools.partial(gather_kernel, n_seq, n_ten), out_shape=...  66.2 us
    pallas_call x1, Pallas kernels, attention(): pl.pallas_call(functools.partial(attention_kernel, n_seq, n_ten), out_sha...  52.7 us
    pallas_call x1, Pallas kernels, scatter(): pl.pallas_call(functools.partial(scatter_kernel, n_seq, n_ten), out_shape...  40.4 us
    unnamed x59, local copies, waits for them, and re-layouts  8.94 us
    dot_general x4, matrix products, nt(): lax.dot_general(a, b, (((1,), (1,)), ((), ())), preferred_element_type=F32)  6.94 us

profile of v1, /device:TPU:1, one launch (start us, length us, event | category | flops | bytes accessed | tf_op | source)
XLA Modules:
  0.0 214.2 jit_solution(9015303118183742539)
XLA Ops:
  0.6 1.4 fusion.62
  4.6 2.7 %fusion.59 = (bf16[256,1,256]{2,1,0:T(2,128)(2,1)S(1)}, bf16[256,1,256]{2,1,0:T(2,128)(2,1)S(1)}, bf16[256,1,256]{2,1,0:T(2,128)(2,1)S(1)}, bf16[256,1,256]{2,1,0:T(2,128)(2,1)S(1)}) fusion(bf16[256,4,256]{2,1,0:T(4,128)(2,1)} %param.12), kind=kLoop, calls=%fused_computation.118 | loop fusion | bytes 1048576 | tf_op jit(solution)/shard_map/slice | solution.py:545
  7.4 0.2 fusion.12
  7.5 0.0 copy-start.17
  7.5 0.0 copy-start.18
  7.5 0.0 copy-start.19
  7.6 0.0 copy-start.20
  7.6 0.0 copy-start.21
  7.6 0.0 copy-start.22
  15.4 0.0 copy-start.1
  15.4 0.2 fusion.16
  15.7 0.1 pad_add_fusion
  16.0 0.6 copy-done.1
  16.7 66.2 %shard_map.155 = (bf16[4,8,2,176,128]{4,3,2,1,0:T(8,128)(2,1)S(1)}, bf16[2,256,2048]{2,1,0:T(8,128)(2,1)S(1)}, bf16[256,2048]{1,0:T(8,128)(2,1)S(1)}) custom-call(bf16[2,176,128]{2,1,0:T(8,128)(2,1)S(1)} %pad_maximum_fusion.5.pay, bf16[256,256]{1,0:T(8,128)(2,1)S(1)} %slice.173.loc, f32[16,256]{1,0:T(8,128)S(1)} %get-tuple-element.70.head, ...), custom_call_target="tpu_custom_call" | custom-call | tf_op jit(solution)/shard_map/pallas_call | solution.py:179
  82.9 1.0 copy-done.4
  83.9 1.6 copy-done.2
  85.5 0.1 copy.119
  85.6 0.1 reshape.269
  85.7 1.9 fusion.57
  87.6 1.0 reshape.270
  88.6 0.8 convolution_convert_fusion.8
  89.4 1.0 reshape.271
  90.4 0.2 convolution_convert_fusion.7
  90.6 0.8 pad_maximum_fusion.6.tkv
  91.4 0.4 convert_reduce_fusion
  91.8 0.7 multiply_reduce_fusion.1
  92.5 0.7 multiply_convert_fusion
  93.2 1.4 copy-done.3
  94.6 1.4 fusion.58
  96.0 0.7 convolution_convert_fusion.4
  96.7 0.1 copy-done.9
  96.8 1.9 maximum_select_fusion
  98.8 0.7 convolution_convert_fusion.3
  99.5 1.6 copy-done.6
  101.1 0.1 copy-done.11
  101.2 0.7 convolution_convert_fusion.6
  101.9 0.7 convolution_convert_fusion.5
  102.6 0.1 pad_maximum_fusion.2
  103.4 52.7 %shard_map.156 = (bf16[512,128]{1,0:T(8,128)(2,1)S(1)}, bf16[512,128]{1,0:T(8,128)(2,1)S(1)}, bf16[512,128]{1,0:T(8,128)(2,1)S(1)}, bf16[512,128]{1,0:T(8,128)(2...) custom-call(bf16[512,256]{1,0:T(8,128)(2,1)S(1)} %get-tuple-element.97.kv, ...), custom_call_target="tpu_custom_call" | custom-call | tf_op jit(solution)/shard_map/pallas_call | solution.py:368
  156.0 0.7 fusion.64
  156.8 0.3 copy-done.10
  157.1 0.7 fusion.63
  157.8 3.8 %multiply_reduce_fusion.2 = (f32[512]{0:T(512)S(1)}, f32[512]{0:T(512)S(1)}, bf16[512,2048]{1,0:T(8,128)(2,1)}, f32[512,2048]{1,0:T(8,128)}) fusion(f32[2048]{0:T(1024)S(1)} %copy-done.16, f32[512]{0:T(512)S(1)} %bitcast.147, f32[512]{0:T(512)S(1)} %bitcast.148, bf16[2,256,2048]{2,1,0:T(8,128)(2,1)S(1)} %get-tuple-element.18, ...), kind=kOutput, calls=%fused_computation.6 | convolution fusion | flops 278920192 | bytes 17448960 | tf_op jit(solution)/shard_map/dot_general | solution.py:25
  161.6 2.9 %copy.74 = bf16[2048,512]{1,0:T(8,128)(2,1)S(1)} copy(bf16[2048,512]{0,1:T(8,128)(2,1)} %bitcast.134) | data formatting | bytes 4194304 | tf_op jit(solution)/shard_map/dot_general | solution.py:33
  164.5 1.5 fusion.6
  166.0 0.2 copy.76
  166.2 0.2 convolution_convert_fusion.1
  166.5 0.1 pad_bitcast_fusion
  166.6 0.2 convolution_convert_fusion.2
  166.8 0.1 pad_bitcast_fusion.1
  166.9 0.2 copy-done.15
  167.1 0.1 pad_maximum_fusion.sg
  167.2 1.1 dynamic_slice.9.unit
  168.3 1.7 convolution_convert_fusion
  170.1 0.1 broadcast_in_dim.41.inv
  170.2 0.1 dynamic_slice.11
  170.3 40.4 %shard_map.157 = (bf16[256,256]{1,0:T(8,128)(2,1)S(1)}, bf16[256,256]{1,0:T(8,128)(2,1)S(1)}, bf16[16,256]{1,0:T(8,128)(2,1)S(1)}, f32[64,256]{1,0:T(8,128)S(1)}) custom-call(bf16[2,256,2048]{2,1,0:T(8,128)(2,1)S(1)} %bitcast.127, bf16[2,256,2048]{2,1,0:T(8,128)(2,1)S(1)} %bitcast.126, bf16[8,4,2,64,128]{4,3,2,1,0:T(8,128)(2,1)S(1)} %pad_maximum_fusion.sg, ...), custom_call_target="tpu_custom_call" | custom-call | tf_op jit(solution)/shard_map/pallas_call | solution.py:491
  210.7 0.1 fusion.38
  210.8 0.2 fusion.41
  211.0 0.1 pad_maximum_fusion.1
  211.1 1.2 copy.81
  212.3 0.6 fusion.61
  212.9 0.6 slice_bitcast_fusion
  213.5 0.7 copy.127
  (62 shorter events, 0.4 us)
Async XLA Ops:
  7.5 8.3 %copy-start.17 = (bf16[32,256]{1,0:T(8,128)(2,1)S(1)}, bf16[32,256]{1,0:T(8,128)(2,1)}, u32[]{:S(2)}) copy-start(bf16[32,256]{1,0:T(8,128)(2,1)} %param.15) | copy-start | bytes 49156
  7.5 8.3 %copy-start.18 = (bf16[32,256]{1,0:T(8,128)(2,1)S(1)}, bf16[32,256]{1,0:T(8,128)(2,1)}, u32[]{:S(2)}) copy-start(bf16[32,256]{1,0:T(8,128)(2,1)} %param.16) | copy-start | bytes 49156
  7.5 8.3 %copy-start.19 = (bf16[32,256]{1,0:T(8,128)(2,1)S(1)}, bf16[32,256]{1,0:T(8,128)(2,1)}, u32[]{:S(2)}) copy-start(bf16[32,256]{1,0:T(8,128)(2,1)} %param.17) | copy-start | bytes 49156
  7.6 8.3 %copy-start.20 = (bf16[256,32]{0,1:T(8,128)(2,1)S(1)}, bf16[256,32]{0,1:T(8,128)(2,1)}, u32[]{:S(2)}) copy-start(bf16[256,32]{0,1:T(8,128)(2,1)} %param.18) | copy-start | bytes 49156
  7.6 8.3 %copy-start.21 = (bf16[12,256]{1,0:T(8,128)(2,1)S(1)}, bf16[12,256]{1,0:T(8,128)(2,1)}, u32[]{:S(2)}) copy-start(bf16[12,256]{1,0:T(8,128)(2,1)} %param.20) | copy-start | bytes 18436
  7.6 8.3 %copy-start.22 = (bf16[12,256]{1,0:T(8,128)(2,1)S(1)}, bf16[12,256]{1,0:T(8,128)(2,1)}, u32[]{:S(2)}) copy-start(bf16[12,256]{1,0:T(8,128)(2,1)} %param.21) | copy-start | bytes 18436
  14.8 1.2 copy-start.23
  15.4 1.2 copy-start.1
  82.9 1.0 copy-start.4
  83.9 1.6 copy-start.2
  85.6 4.8 %copy-start.13 = (bf16[128,768]{1,0:T(8,128)(2,1)}, bf16[128,768]{1,0:T(8,128)(2,1)S(1)}, u32[]{:S(2)}) copy-start(bf16[128,768]{1,0:T(8,128)(2,1)S(1)} %reshape.269) | copy-start | bytes 589828
  91.4 1.1 copy-start.16
  92.5 2.2 %copy-start.3 = (bf16[4,8,2,176,128]{4,3,2,1,0:T(8,128)(2,1)S(1)}, bf16[4,8,2,176,128]{4,3,2,1,0:T(8,128)(2,1)}, u32[]{:S(2)}) copy-start(bf16[4,8,2,176,128]{4,3,2,1,0:T(8,128)(2,1)} %copy-done.2) | copy-start | bytes 8650756
  93.2 2.8 %copy-start.5 = (bf16[2,256,2048]{2,1,0:T(8,128)(2,1)}, bf16[2,256,2048]{2,1,0:T(8,128)(2,1)S(1)}, u32[]{:S(2)}) copy-start(bf16[2,256,2048]{2,1,0:T(8,128)(2,1)S(1)} %multiply_convert_fusion) | copy-start | bytes 6291460
  96.0 0.8 copy-start.9
  96.8 2.0 copy-start.12
  98.7 58.0 %copy-start.7 = (bf16[2,256,2048]{2,1,0:T(8,128)(2,1)}, bf16[2,256,2048]{2,1,0:T(8,128)(2,1)S(1)}, u32[]{:S(2)}) copy-start(bf16[2,256,2048]{2,1,0:T(8,128)(2,1)S(1)} %maximum_select_fusion) | copy-start | bytes 6291460
  98.8 2.3 %copy-start.6 = (bf16[2,256,2048]{2,1,0:T(8,128)(2,1)S(1)}, bf16[2,256,2048]{2,1,0:T(8,128)(2,1)}, u32[]{:S(2)}) copy-start(bf16[2,256,2048]{2,1,0:T(8,128)(2,1)} %copy-done.5) | copy-start | bytes 6291460
  98.8 2.4 %copy-start.11 = (bf16[4,8,2,32,128]{4,3,2,1,0:T(8,128)(2,1)S(1)}, bf16[4,8,2,32,128]{4,3,2,1,0:T(8,128)(2,1)}, u32[]{:S(2)}) copy-start(bf16[4,8,2,32,128]{4,3,2,1,0:T(8,128)(2,1)} %get-tuple-element.67) | copy-start | bytes 1572868
  98.8 3.1 %copy-start.8 = (bf16[4,8,2,32,128]{4,3,2,1,0:T(8,128)(2,1)S(1)}, bf16[4,8,2,32,128]{4,3,2,1,0:T(8,128)(2,1)}, u32[]{:S(2)}) copy-start(bf16[4,8,2,32,128]{4,3,2,1,0:T(8,128)(2,1)} %get-tuple-element.66) | copy-start | bytes 1572868
  156.0 1.0 copy-start.10
  164.5 1.5 copy-start.14
  166.0 1.0 copy-start.15
  167.2 3.1 %copy-start = (bf16[512,2048]{1,0:T(8,128)(2,1)S(1)}, bf16[512,2048]{1,0:T(8,128)(2,1)}, u32[]{:S(2)}) copy-start(bf16[512,2048]{1,0:T(8,128)(2,1)} %get-tuple-element.61) | copy-start | bytes 6291460

commit v2 on v1

v2 whole, which is shorter than its diff:
```python
import functools

import jax
import jax.numpy as jnp
from jax import lax
from jax.experimental import pallas as pl
from jax.experimental.pallas import tpu as pltpu
from jax.sharding import PartitionSpec as P

HD = 64
WINDOW = 1500
EPS = 1e-05
RING = 8
MESH = pl.DeviceIdType.MESH
BF = jnp.bfloat16
F32 = jnp.float32


def dims_of(n_seq):
    z = min(RING, n_seq // 2)
    return n_seq // (2 * z), z


def nt(a, b):
    return lax.dot_general(a, b, (((1,), (1,)), ((), ())), preferred_element_type=F32)


def nn(a, b):
    return lax.dot_general(a, b, (((1,), (0,)), ((), ())), preferred_element_type=F32)


def tn(a, b):
    return lax.dot_general(a, b, (((0,), (0,)), ((), ())), preferred_element_type=F32)


def send(src, dst, ssem, rsem, seq, ten):
    return pltpu.make_async_remote_copy(
        src_ref=src, dst_ref=dst, send_sem=ssem, recv_sem=rsem, device_id=(seq, ten), device_id_type=MESH
    )


def greet(partners):
    sem = pltpu.get_barrier_semaphore()
    for seq, ten in partners:
        pl.semaphore_signal(sem, inc=1, device_id=(seq, ten), device_id_type=MESH)
    pl.semaphore_wait(sem, len(partners))


class Place:
    def __init__(self, n_seq, n_ten):
        self.n_seq, self.n_ten = n_seq, n_ten
        self.H, self.Z = dims_of(n_seq)
        self.s = lax.axis_index("seq")
        self.t = lax.axis_index("tensor")
        self.c = lax.rem(self.s, 2)
        self.p = lax.div(self.s, 2)
        self.h = lax.div(self.p, self.Z)
        self.z = lax.rem(self.p, self.Z)
        self.chips = n_seq // 2

    def seq(self, h, z, c):
        return (h * self.Z + z) * 2 + c

    def sibling(self):
        return self.seq(self.h, self.z, 1 - self.c)

    def chip(self, k):
        return lax.rem(self.p + k + self.chips, self.chips) * 2 + self.c

    def other_h(self, d):
        return lax.rem(self.h + d, self.H)

    def other_z(self, d):
        return lax.rem(self.z + d + self.Z, self.Z)

    def other_t(self, d):
        return lax.rem(self.t + d + self.n_ten, self.n_ten)

    def next(self, d):
        return lax.rem(self.s + d + self.n_seq, self.n_seq)


def fused_kernel(
    n_seq, n_ten, delays, text_len, pay, emb, gain, cot, out, de, sgo,
    g, f, cots, rimbuf, blk, longer, nst, normed, states32, states,
    kv, qd, tkv, kx, qx, wbuf, wtbuf, mixbuf, totbuf, st, cstat,
    att, dq, dk, dv, tkg, tvg,
    opt, opx, opr, ipt, ipx, ipr, ops, ips, nst_out, nsx, nss, nsr,
    sga, sgza, sgb, sgzb, sgh, sghr, sgs, sgx, fg, rim,
    lsem, one_s, one_r, h_s, h_r, z_s, z_r, f_s, f_r, x_s, x_r,
    k_s, k_r, q_s, q_r, t_s, t_r, ox_s, ox_r, ix_s, ix_r, o_s, o_r, i_s, i_r, n_s, n_r,
    za_s, za_r, zb_s, zb_r, hh_s, hh_r,
):
    me = Place(n_seq, n_ten)
    H, Z, T = me.H, me.Z, n_ten
    s, t, c, h, z, p = me.s, me.t, me.c, me.h, me.z, me.p
    sib = me.sibling()
    half = Z // 2
    width = emb.shape[2]
    Q = emb.shape[1]
    B = 2 * Q
    R = sga.shape[3]
    text = states.shape[0]
    full = width * T
    scale = HD ** (-0.5)
    zero = jnp.zeros((), BF)
    right, left = me.seq(h, me.other_z(1), c), me.seq(h, me.other_z(-1), c)
    partners = [(sib, t), (me.next(1), t), (me.next(-1), t)]
    partners += [(me.seq(me.other_h(d), z, c), t) for d in range(1, H)]
    partners += [(me.seq(h, me.other_z(d), c), t) for d in range(1, Z)]
    partners += [(s, me.other_t(d)) for d in range(1, T)]
    partners += [(me.chip(k), t) for k in (1, -1, 2, -2, 3, -3)]
    greet(partners)
    outgoing = []

    def go(copy):
        copy.start()
        outgoing.append(copy)

    def half_rows(core):
        return pl.ds(pl.multiple_of(core * Q, Q), Q)

    go(send(pay.at[1 - c], g.at[p, c], one_s.at[0], one_r.at[0], sib, t))
    mine = pltpu.make_async_copy(pay.at[c], g.at[p, c], lsem.at[0])
    mine.start()
    longer[...] = jnp.zeros_like(longer)
    for d in range(4):
        book = jnp.zeros((Q, width), F32)
        for k in range(4):
            book = book + jnp.where(delays[k] == d, emb[k].astype(F32), 0.0)
        longer[d : d + Q, :] = longer[d : d + Q, :] + book
    go(send(longer.at[pl.ds(Q, 16)], rimbuf, one_s.at[1], one_r.at[1], me.next(1), t))
    mine.wait()
    send(pay.at[c], g.at[p, 1 - c], one_s.at[0], one_r.at[0], sib, t).wait_recv()
    for d in range(1, H):
        go(send(g.at[p], g.at[p], h_s.at[d], h_r.at[d], me.seq(me.other_h(d), z, c), t))

    def step(way, k, d):
        hh = me.other_h(d)
        zz = me.other_z(-(k - 1) if way == 0 else k - 1)
        go(send(g.at[hh * Z + zz], g.at[hh * Z + zz], z_s.at[way, k, d], z_r.at[way, k, d], right if way == 0 else left, t))

    def arrived(way, k, d):
        hh = me.other_h(d)
        zz = me.other_z(-k if way == 0 else k)
        send(g.at[hh * Z + zz], g.at[hh * Z + zz], z_s.at[way, k, d], z_r.at[way, k, d], right, t).wait_recv()

    def used(way, k, d):
        if k < half:
            return True
        if k > half:
            return False
        return (d < H // 2) if way == 0 else (d >= H // 2)

    for way in (0, 1):
        if used(way, 1, 0):
            step(way, 1, 0)
    send(longer.at[pl.ds(Q, 16)], rimbuf, one_s.at[1], one_r.at[1], me.next(1), t).wait_recv()
    blk[...] = longer[0:Q, :].astype(BF)
    blk[0:16, :] = (longer[0:16, :] + jnp.where(s > 0, rimbuf[...], 0.0)).astype(BF)
    for d in range(1, T):
        go(send(blk, f.at[c, t], f_s.at[d], f_r.at[d], s, me.other_t(d)))
    go(send(blk, f.at[c, t], x_s.at[0], x_r.at[0], sib, t))
    own = pltpu.make_async_copy(blk, f.at[c, t], lsem.at[1])
    own.start()
    for d in range(1, H):
        hh = me.other_h(H - d)
        send(g.at[hh * Z + z], g.at[hh * Z + z], h_s.at[d], h_r.at[d], sib, t).wait_recv()
        for way in (0, 1):
            if used(way, 1, H - d):
                step(way, 1, H - d)
    go(send(cot, cots.at[half_rows(c)], one_s.at[2], one_r.at[2], sib, t))
    mycot = pltpu.make_async_copy(cot, cots.at[half_rows(c)], lsem.at[2])
    mycot.start()
    order = [0] + [H - e for e in range(1, H)]
    ring_last = half

    def ring(k):
        for d in order:
            for way in (0, 1):
                if used(way, k, d):
                    arrived(way, k, d)
                    if used(way, k + 1, d):
                        step(way, k + 1, d)

    def pass_frames():
        for d in range(1, T):
            tt = me.other_t(-d)
            send(blk, f.at[c, tt], f_s.at[d], f_r.at[d], sib, t).wait_recv()
            go(send(f.at[c, tt], f.at[c, tt], x_s.at[d], x_r.at[d], sib, t))

    def norm(cc):
        def fold(v):
            return v[:, 0:128] + v[:, 128:256]

        acc = jnp.zeros((Q, 128), F32)
        acc = lax.fori_loop(0, T, lambda i, a: a + fold(f[cc, i].astype(F32)), acc)
        mean = jnp.sum(acc, 1, keepdims=True) / full

        def second(i, a):
            v = f[cc, i].astype(F32) - mean
            return a + fold(v * v)

        acc = lax.fori_loop(0, T, second, jnp.zeros((Q, 128), F32))
        inv = lax.rsqrt(jnp.sum(acc, 1, keepdims=True) / full + EPS)
        lane128 = lax.broadcasted_iota(jnp.int32, (Q, 128), 1)
        nst[cc] = jnp.where(lane128 == 0, mean, inv)

        def third(i, carry):
            w = pl.ds(pl.multiple_of(i * width, width), width)
            v = (f[cc, i].astype(F32) - mean) * inv
            normed[half_rows(cc), w] = (v * gain[0:1, w]).astype(BF)
            return carry

        lax.fori_loop(0, T, third, 0)

    for k in range(1, half):
        if k == max(half - 2, 1):
            pass_frames()
        ring(k)
    if half == 1:
        pass_frames()
    own.wait()
    norm(c)
    for d in range(T):
        tt = me.other_t(-d)
        send(blk, f.at[1 - c, tt], x_s.at[d], x_r.at[d], sib, t).wait_recv()
    norm(1 - c)
    ring(half)

    def weight(i):
        return g[:, :, i * R : (i + 1) * R, :].reshape(n_seq * R, 128)

    def project(src, i, dst, lanes):
        def go_rows(rb, carry):
            rows = half_rows(rb)
            dst[rows, lanes] = nn(src[rows, :], weight(i)).astype(BF)
            return carry

        lax.fori_loop(0, 2, go_rows, 0)

    lo, hi = slice(0, 128), slice(128, 256)

    def kslot(k):
        return kx.at[pl.ds((3 - k) * B, B)]

    def qslot(k):
        return qx.at[pl.ds(k * B, B)]

    project(normed, 1, kv, lo)
    project(normed, 2, kv, hi)
    go(send(kv, kslot(1), k_s.at[0], k_r.at[0], me.chip(1), t))
    project(normed, 0, qd, lo)
    mycot.wait()
    send(cot, cots.at[half_rows(c)], one_s.at[2], one_r.at[2], sib, t).wait_recv()
    project(cots, 3, qd, hi)
    go(send(qd, qslot(1), q_s.at[0], q_r.at[0], me.chip(-1), t))
    kx[pl.ds(3 * B, B), :] = kv[...]
    qx[pl.ds(0, B), :] = qd[...]

    states32[...] = g[:, :, 4 * R + 32 : 4 * R + 48, :].reshape(n_seq, 16, 128).astype(F32)
    per = text // n_seq
    qn = 16 // per
    for r in range(per):
        for qq in range(qn):
            states[r * n_seq : (r + 1) * n_seq, qq * 128 : (qq + 1) * 128] = states32[:, r * qn + qq, :].astype(BF)
    for i in range(2):
        w = g[:, :, 4 * R + 16 * i : 4 * R + 16 * (i + 1), :].reshape(n_seq * 16, 128)
        tkv[:, i * 128 : (i + 1) * 128] = nn(states[...], w).astype(BF)
    token = lax.broadcasted_iota(jnp.int32, (1, text), 1)
    live = lax.rem(token, n_seq) * per + lax.div(token, n_seq) < text_len[0]

    lane = lax.broadcasted_iota(jnp.int32, (Q, 128), 1)
    row = lax.broadcasted_iota(jnp.int32, (Q, Q), 0)
    col = lax.broadcasted_iota(jnp.int32, (Q, Q), 1)
    heads = [lane < HD, lane >= HD]
    chunks = (WINDOW + Q - 2) // Q + 1
    lead = (chunks - 1) * Q

    def forward_chunk(qb, hd, q, j):
        base = pl.multiple_of((qb + j) * Q, Q)
        w = jnp.exp(nt(q, kx[pl.ds(base, Q), lo]))
        ok = p * B - 3 * B + (qb + j) * Q >= 0
        if lead - j * Q + Q - 1 >= WINDOW:
            ok = ok & (lead + row - j * Q - col < WINDOW)
        if j == chunks - 1:
            ok = ok & (col <= row)
        w = jnp.where(ok, w, 0.0)
        wbuf[qb, hd, j] = w
        return w[:, 0:128] + w[:, 128:256], nn(w.astype(BF), kx[pl.ds(base, Q), hi])

    def forward(k):
        for qb in range(2):
            q_both = qd[qb * Q : (qb + 1) * Q, lo]
            for hd in range(2):
                q = jnp.where(heads[hd], q_both, zero) * jnp.asarray(scale, BF)
                if k == 0:
                    wt = jnp.where(live, jnp.exp(nt(q, tkv[:, lo])), 0.0)
                    wtbuf[qb, hd] = wt
                    total, mix = wt, nn(wt.astype(BF), tkv[:, hi])
                else:
                    total, mix = totbuf[qb, hd], mixbuf[qb, hd]
                for j in range(chunks):
                    if (qb + j) // 2 == 3 - k:
                        a, b = forward_chunk(qb, hd, q, j)
                        total, mix = total + a, mix + b
                totbuf[qb, hd], mixbuf[qb, hd] = total, mix

    def pass_keys(k):
        send(kv, kslot(k), k_s.at[k - 1], k_r.at[k - 1], me.chip(1), t).wait_recv()
        if k < 3:
            go(send(kslot(k), kslot(k + 1), k_s.at[k], k_r.at[k], me.chip(1), t))

    def pass_queries(k):
        send(qd, qslot(k), q_s.at[k - 1], q_r.at[k - 1], me.chip(-1), t).wait_recv()
        if k < 3:
            go(send(qslot(k), qslot(k + 1), q_s.at[k], q_r.at[k], me.chip(-1), t))

    forward(0)
    for k in (1, 2, 3):
        pass_keys(k)
        pass_queries(k)
        forward(k)
    for qb in range(2):
        rows = slice(qb * Q, (qb + 1) * Q)
        d_both = qd[rows, hi].astype(F32)
        parts, stats = [], []
        for hd in range(2):
            total = jnp.sum(totbuf[qb, hd], 1, keepdims=True)
            a_head = (mixbuf[qb, hd] / total).astype(BF)
            parts.append(a_head)
            inner = jnp.sum(jnp.where(heads[hd], d_both * a_head.astype(F32), 0.0), 1, keepdims=True)
            stats.append((1.0 / total, inner))
        att[rows, :] = jnp.where(heads[0], parts[0], parts[1])
        (r0, i0), (r1, i1) = stats
        packed = jnp.where(lane == 0, r0, jnp.where(lane == 1, r1, jnp.where(lane == 2, i0, i1)))
        cstat[rows, :] = packed
        st[0, :, rows] = packed.T[0:8, :]
    for k in (1, 2, 3):
        go(send(st.at[0], st.at[k], t_s.at[k], t_r.at[k], me.chip(-k), t))

    def w_block(i, tt):
        n = width // (2 * R)
        return g[pl.ds(tt * n, n), :, i * R : (i + 1) * R, :].reshape(width, 128)

    for d in range(T):
        tt = me.other_t(d)
        opt[d] = nt(att[half_rows(1 - c), :], w_block(3, tt)).astype(BF)
        go(send(opt.at[d], opx.at[d], ox_s.at[d], ox_r.at[d], sib, t))
    for e in range(full // B):
        piece = tn(att[...], cots[:, e * B : (e + 1) * B])
        n = B // R
        for a in range(B // 128):
            rows = piece[:, a * 128 : (a + 1) * 128].T.astype(BF).reshape(128 // R, R, 128)
            for b in range(128 // R):
                who = e * n + a * (128 // R) + b
                hh, zz, cc = who // (2 * Z), (who // 2) % Z, who % 2
                sga[zz, hh, cc] = rows[b]
    for d in range(1, Z):
        zz = me.other_z(d)
        go(send(sga.at[zz], sgza.at[d], za_s.at[d], za_r.at[d], me.seq(h, zz, c), t))

    tkg[...] = jnp.zeros_like(tkg)
    tvg[...] = jnp.zeros_like(tvg)

    def query_grads(qb, carry):
        rows = half_rows(qb)
        q_both = qd[rows, lo]
        d_both = qd[rows, hi]
        parts = []
        for hd in range(2):
            q = jnp.where(heads[hd], q_both, zero)
            d = jnp.where(heads[hd], d_both, zero)
            r = cstat[rows, hd : hd + 1]
            inner = cstat[rows, 2 + hd : 3 + hd]
            sh = wtbuf[qb, hd] * r
            ds = (sh * (nt(d, tkv[:, hi]) - inner)).astype(BF)
            grad = nn(ds, tkv[:, lo])
            tkg[...] += tn(ds, q) * scale
            tvg[...] += tn(sh.astype(BF), d)
            for j in range(chunks):
                base = pl.multiple_of((qb + j) * Q, Q)
                keys = kx[pl.ds(base, Q), :]
                ds = (wbuf[qb, hd, j] * r * (nt(d, keys[:, hi]) - inner)).astype(BF)
                grad = grad + nn(ds, keys[:, lo])
            parts.append(grad)
        dq[rows, :] = (jnp.where(heads[0], parts[0], parts[1]) * scale).astype(BF)
        return carry

    lax.fori_loop(0, 2, query_grads, 0)
    for i, grad in enumerate((tkg, tvg)):
        piece = tn(states[...], grad[...].astype(BF)).astype(BF).reshape(H, Z, 2, 16, 128)
        for zz in range(Z):
            sgb[zz, :, :, 16 * i : 16 * (i + 1), :] = piece[:, zz]
    for d in range(1, Z):
        zz = me.other_z(d)
        go(send(sgb.at[zz], sgzb.at[d], zb_s.at[d], zb_r.at[d], me.seq(h, zz, c), t))
    for d in [*range(1, T), 0]:
        tt = me.other_t(d)
        send(opt.at[d], opx.at[d], ox_s.at[d], ox_r.at[d], sib, t).wait_recv()
        ops[d] = (nt(att[half_rows(c), :], w_block(3, tt)) + opx[d].astype(F32)).astype(BF)
        if d:
            go(send(ops.at[d], opr.at[d], o_s.at[d], o_r.at[d], s, tt))
    for k in (1, 2, 3):
        send(st.at[0], st.at[k], t_s.at[k], t_r.at[k], me.chip(-k), t).wait_recv()

    def key_grads(kb, carry):
        rows = half_rows(kb)
        k_both = kv[rows, lo]
        v_both = kv[rows, hi]
        kparts, vparts = [], []
        for hd in range(2):
            kh = jnp.where(heads[hd], k_both, zero) * jnp.asarray(scale, BF)
            vh = jnp.where(heads[hd], v_both, zero)
            gk = jnp.zeros((Q, 128), F32)
            gv = jnp.zeros((Q, 128), F32)
            for i in range(chunks):
                base = pl.multiple_of((kb + i) * Q, Q)
                qs = qx[pl.ds(base, Q), :]
                at = lax.div(kb + i, 2)
                part = pl.ds(pl.multiple_of(lax.rem(kb + i, 2) * Q, Q), Q)
                r = st[at, hd : hd + 1, part]
                inner = st[at, 2 + hd : 3 + hd, part]
                ok = p * B + (kb + i) * Q < n_seq * Q
                if i == 0:
                    ok = ok & (col >= row)
                if i * Q + Q - 1 >= WINDOW:
                    ok = ok & (i * Q + col - row < WINDOW)
                sh = jnp.where(ok, jnp.exp(nt(kh, qs[:, lo])) * r, 0.0)
                ds = (sh * (nt(vh, qs[:, hi]) - inner)).astype(BF)
                gv = gv + nn(sh.astype(BF), qs[:, hi])
                gk = gk + nn(ds, qs[:, lo])
            kparts.append(gk)
            vparts.append(gv)
        dk[rows, :] = (jnp.where(heads[0], kparts[0], kparts[1]) * scale).astype(BF)
        dv[rows, :] = jnp.where(heads[0], vparts[0], vparts[1]).astype(BF)
        return carry

    lax.fori_loop(0, 2, key_grads, 0)

    def input_block(cc, tt):
        rows = half_rows(cc)
        grad = nt(dq[rows, :], w_block(0, tt)) + nt(dk[rows, :], w_block(1, tt)) + nt(dv[rows, :], w_block(2, tt))
        lanes = pl.ds(pl.multiple_of(tt * width, width), width)
        scaled = grad * gain[0:1, lanes]
        unit = (f[cc, tt].astype(F32) - nst[cc, :, 0:1]) * nst[cc, :, 1:2]
        both = scaled * unit
        return grad, scaled[:, 0:128] + scaled[:, 128:256], both[:, 0:128] + both[:, 128:256]

    def pack_sums(plain, unit):
        plain = jnp.sum(plain, 1, keepdims=True)
        unit = jnp.sum(unit, 1, keepdims=True)
        return jnp.where(lane == 0, plain, unit).T[0:8, :]

    plain = jnp.zeros((Q, 128), F32)
    unit = jnp.zeros((Q, 128), F32)
    for d in [*range(1, T), 0]:
        tt = me.other_t(d)
        grad, a, b = input_block(1 - c, tt)
        plain, unit = plain + a, unit + b
        ipt[d] = grad.astype(BF)
        go(send(ipt.at[d], ipx.at[d], ix_s.at[d], ix_r.at[d], sib, t))
    nst_out[...] = pack_sums(plain, unit)
    go(send(nst_out, nsx, n_s.at[0], n_r.at[0], sib, t))
    plain = jnp.zeros((Q, 128), F32)
    unit = jnp.zeros((Q, 128), F32)
    for d in [*range(1, T), 0]:
        tt = me.other_t(d)
        grad, a, b = input_block(c, tt)
        plain, unit = plain + a, unit + b
        send(ipt.at[d], ipx.at[d], ix_s.at[d], ix_r.at[d], sib, t).wait_recv()
        ips[d] = (grad + ipx[d].astype(F32)).astype(BF)
        if d:
            go(send(ips.at[d], ipr.at[d], i_s.at[d], i_r.at[d], s, tt))
    send(nst_out, nsx, n_s.at[0], n_r.at[0], sib, t).wait_recv()
    nss[...] = pack_sums(plain, unit) + nsx[...]
    for d in range(1, T):
        go(send(nss, nsr.at[d], n_s.at[d], n_r.at[d], s, me.other_t(d)))

    acc_a = sga[z].astype(F32)
    acc_b = sgb[z].astype(F32)
    for d in range(1, Z):
        send(sga.at[0], sgza.at[d], za_s.at[d], za_r.at[d], sib, t).wait_recv()
        send(sgb.at[0], sgzb.at[d], zb_s.at[d], zb_r.at[d], sib, t).wait_recv()
        acc_a = acc_a + sgza[d].astype(F32)
        acc_b = acc_b + sgzb[d].astype(F32)
    sgh[:, :, 0:R, :] = acc_a
    sgh[:, :, R : R + 32, :] = acc_b
    for d in range(1, H):
        hh = me.other_h(d)
        go(send(sgh.at[hh], sghr.at[d], hh_s.at[d], hh_r.at[d], me.seq(hh, z, c), t))

    total = ips[0].astype(F32)
    sums = nss[...]
    for d in range(1, T):
        send(nss, nsr.at[d], n_s.at[d], n_r.at[d], sib, t).wait_recv()
        sums = sums + nsr[d]
        send(ips.at[d], ipr.at[d], i_s.at[d], i_r.at[d], sib, t).wait_recv()
        total = total + ipr[d].astype(F32)
    tall = jnp.concatenate([sums] * 16, 0).T
    here = pl.ds(pl.multiple_of(t * width, width), width)
    inv = nst[c, :, 1:2]
    unit = (f[c, t].astype(F32) - nst[c, :, 0:1]) * inv
    grad = inv * (total * gain[0:1, here] - tall[:, 0:1] / full - unit * (tall[:, 1:2] / full))
    fg[...] = grad.astype(BF)
    go(send(fg.at[pl.ds(0, 16)], rim, one_s.at[3], one_r.at[3], me.next(-1), t))
    acc = sgh[h]
    for d in range(1, H):
        send(sgh.at[0], sghr.at[d], hh_s.at[d], hh_r.at[d], sib, t).wait_recv()
        acc = acc + sghr[d]
    sgs[...] = acc
    go(send(sgs.at[1 - c], sgx, one_s.at[4], one_r.at[4], sib, t))
    longer[0:Q, :] = fg[...].astype(F32)
    total = ops[0].astype(F32)
    for d in range(1, T):
        send(ops.at[d], opr.at[d], o_s.at[d], o_r.at[d], sib, t).wait_recv()
        total = total + opr[d].astype(F32)
    out[...] = total.astype(BF)
    send(fg.at[pl.ds(0, 16)], rim, one_s.at[3], one_r.at[3], sib, t).wait_recv()
    send(sgs.at[0], sgx, one_s.at[4], one_r.at[4], sib, t).wait_recv()
    sgo[:, lo] = jnp.where(c == 0, sgs[c], sgx[...])
    sgo[:, hi] = jnp.where(c == 0, sgx[...], sgs[c])
    for copy in outgoing:
        copy.wait_send()
    longer[Q : Q + 16, :] = jnp.where(s < n_seq - 1, rim[...].astype(F32), 0.0)
    for k in range(4):
        book = jnp.zeros((Q, width), F32)
        for d in range(4):
            book = jnp.where(delays[k] == d, longer[d : d + Q, :], book)
        de[k] = book.astype(BF)


def fused(n_seq, n_ten, delays, text_len, pay, emb, gain, cot, text):
    H, Z = dims_of(n_seq)
    T = n_ten
    _, Q, W = emb.shape
    B = 2 * Q
    full = W * T
    R = (pay.shape[1] - 48) // 4
    chunks = (WINDOW + Q - 2) // Q + 1
    dma = pltpu.SemaphoreType.DMA
    vm = pl.BlockSpec(memory_space=pltpu.VMEM)
    sm = pl.BlockSpec(memory_space=pltpu.SMEM)
    V = pltpu.VMEM
    block = V((T, Q, W), BF)
    rows = V((B, 128), BF)
    small = V((text, 128), F32)
    sums = V((8, Q), F32)

    def pair(*shape):
        return [dma(shape), dma(shape)]

    return pl.pallas_call(
        functools.partial(fused_kernel, n_seq, n_ten),
        out_shape=(
            jax.ShapeDtypeStruct((Q, W), BF),
            jax.ShapeDtypeStruct((4, Q, W), BF),
            jax.ShapeDtypeStruct((R + 32, 256), F32),
        ),
        in_specs=[sm, sm, vm, vm, vm, pl.BlockSpec(memory_space=pl.ANY)],
        out_specs=(vm,) * 3,
        scratch_shapes=[
            V((H * Z,) + pay.shape, BF), V((2, T, Q, W), BF), V((B, full), BF), V((16, W), F32), V((Q, W), BF),
            V((Q + 16, W), F32), V((2, Q, 128), F32), V((B, full), BF), V((n_seq, 16, 128), F32),
            V((text, n_seq * 16), BF),
            V((B, 256), BF), V((B, 256), BF), V((text, 256), BF), V((4 * B, 256), BF), V((4 * B, 256), BF),
            V((2, 2, chunks, Q, Q), F32), V((2, 2, Q, text), F32), V((2, 2, Q, 128), F32), V((2, 2, Q, 128), F32),
            V((4, 8, B), F32), V((B, 128), F32),
            rows, rows, rows, rows, small, small,
            block, block, block, block, block, block, block, block, sums, sums, sums, V((T, 8, Q), F32),
            V((Z, H, 2, R, 128), BF), V((Z, H, 2, R, 128), BF), V((Z, H, 2, 32, 128), BF), V((Z, H, 2, 32, 128), BF),
            V((H, 2, R + 32, 128), F32), V((H, 2, R + 32, 128), F32), V((2, R + 32, 128), F32), V((R + 32, 128), F32),
            V((Q, W), BF), V((16, W), BF),
            dma((3,)), *pair(5), *pair(H), *pair(2, Z // 2 + 1, H), *pair(T), *pair(T),
            *pair(3), *pair(3), *pair(4), *pair(T), *pair(T), *pair(T), *pair(T), *pair(T),
            *pair(Z), *pair(Z), *pair(H),
        ],
        compiler_params=pltpu.CompilerParams(collective_id=0, has_side_effects=True, vmem_limit_bytes=56 << 20),
    )(delays, text_len, pay, emb, gain, cot)


def shards(
    n_seq, n_ten, embedded, delays, norm_gain, w_query, w_key, w_value, w_out,
    text_states, w_text_key, w_text_value, text_len, cotangent,
):
    R = w_query.shape[0]
    tr = w_text_key.shape[0]
    per = text_states.shape[0]
    states = jnp.pad(text_states.reshape(per, n_seq, tr), ((0, 0), (0, 0), (0, 16 - tr))).reshape(16, 128)
    pieces = [w_query, w_key, w_value, w_out.T]
    pieces += [jnp.pad(w, ((0, 16 - tr), (0, 0))) for w in (w_text_key, w_text_value)]
    pay = jnp.concatenate(pieces, 0)
    pay = jnp.stack([jnp.concatenate([pay[:, i * 128 : (i + 1) * 128], states], 0) for i in range(2)], 0)
    out, de, sgo = fused(
        n_seq, n_ten, delays, text_len, pay, embedded.transpose(1, 0, 2), norm_gain.reshape(1, -1),
        cotangent, per * n_seq,
    )
    return (out, de.transpose(1, 0, 2), sgo[:R].T, sgo[R : R + tr], sgo[R + 16 : R + 16 + tr])


def solution(mesh):
    placed = (
        P("seq", None, "tensor"), P(), P(),
        P("seq", "tensor"), P("seq", "tensor"), P("seq", "tensor"), P("tensor", "seq"),
        P("seq", None), P("seq", "tensor"), P("seq", "tensor"), P(), P("seq", None),
    )
    return jax.shard_map(
        functools.partial(shards, mesh.shape["seq"], mesh.shape["tensor"]),
        mesh=mesh,
        in_specs=placed,
        out_specs=(
            P("seq", "tensor"), P("seq", None, "tensor"), P("tensor", "seq"),
            P("seq", "tensor"), P("seq", "tensor"),
        ),
        check_vma=False,
    )
```

time: 215 us -> 150 us (0.70)
  the two profiles are of different devices: /device:TPU:1 before, /device:TPU:201 now
where the time goes in v2:
time: 150 us; the launch traced here: 149 us
  Pallas kernels  137 us (91%)
  local copies, waits for them, and re-layouts  9.55 us (6%)
    pallas_call x1, Pallas kernels, fused(): pl.pallas_call(functools.partial(fused_kernel, n_seq, n_ten), out_shape=(...  137 us
    unnamed x16, local copies, waits for them, and re-layouts  7.39 us

profile of v2, /device:TPU:201, one launch (start us, length us, event | category | flops | bytes accessed | tf_op | source)
XLA Modules:
  0.0 149.1 jit_solution(162403742478699188)
XLA Ops:
  0.6 0.0 copy-start.3
  0.6 0.0 copy-start
  1.4 0.0 copy-done.3
  1.4 0.1 reshape.19
  1.5 0.1 reshape.20
  1.6 0.7 constant_dynamic-update-slice_fusion.4
  2.3 0.7 constant_dynamic-update-slice_fusion.3
  3.0 0.7 constant_dynamic-update-slice_fusion.2
  3.8 0.7 bitcast_dynamic-update-slice_fusion
  4.5 0.7 constant_dynamic-update-slice_fusion.1
  5.2 0.7 constant_dynamic-update-slice_fusion
  5.9 0.6 pad_maximum_fusion.pay
  6.6 0.0 copy-done
  6.6 0.9 copy.22
  7.4 137.5 %shard_map.155 = (bf16[256,256]{1,0:T(8,128)(2,1)}, bf16[4,256,256]{2,1,0:T(8,128)(2,1)}, f32[64,256]{1,0:T(8,128)}) custom-call(s32[4]{0:T(128)} %delays.1, s32[1]{0:T(128)S(6)} %copy.29.text_len, bf16[2,176,128]{2,1,0:T(8,128)(2,1)} %pad_maximum_fusion.pay, bf16[4,256,256]{2,1,0:T(8,128)(2,1)} %bitcast.13, f32[1,2048]{1,0:T(1,128)} %bitcast.15, ...), custom_call_target="tpu_custom_call" | custom-call | tf_op jit(solution)/shard_map/pallas_call | solution.py:553
  144.9 0.0 copy-start.2
  144.9 2.3 %copy.20 = bf16[256,4,256]{2,1,0:T(4,128)(2,1)} copy(bf16[256,4,256]{2,0,1:T(8,128)(2,1)} %bitcast.14) | data formatting | bytes 1048576
  147.2 0.0 copy-done.2
  147.2 0.0 copy-start.1
  147.2 0.6 slice_bitcast_fusion
  147.8 0.6 fusion.3
  148.4 0.0 copy-done.1
  148.4 0.7 copy.30
  (3 shorter events, 0.0 us)
Async XLA Ops:
  0.6 0.7 copy-start.3
  0.6 5.9 %copy-start = (bf16[256,4,256]{2,1,0:T(4,128)(2,1)S(1)}, bf16[256,4,256]{2,1,0:T(4,128)(2,1)}, u32[]{:S(2)}) copy-start(bf16[256,4,256]{2,1,0:T(4,128)(2,1)} %param.12) | copy-start | bytes 1572868
  144.9 2.3 %copy-start.2 = (f32[64,256]{1,0:T(8,128)S(1)}, f32[64,256]{1,0:T(8,128)}, u32[]{:S(2)}) copy-start(f32[64,256]{1,0:T(8,128)} %get-tuple-element.10) | copy-start | bytes 196612
  147.2 1.2 copy-start.1

commit v3 on v2

--- a/solution.py
+++ b/solution.py
@@ -11,6 +11,7 @@
 WINDOW = 1500
 EPS = 1e-05
 RING = 8
+RELAY = 1
 MESH = pl.DeviceIdType.MESH
 BF = jnp.bfloat16
 F32 = jnp.float32
@@ -80,15 +81,77 @@
         return lax.rem(self.s + d + self.n_seq, self.n_seq)
 
 
+class Chain:
+    def __init__(self, me, sign, at, relay, ss, rr, rs, rx):
+        self.me, self.sign, self.at, self.relay, self.ss, self.rr, self.rs, self.rx = me, sign, at, relay, ss, rr, rs, rx
+        self.edge, self.turn = (me.Z - 1, 0) if sign > 0 else (0, me.Z - 1)
+        row = me.other_h(sign + me.H)
+        if RELAY == 1:
+            self.at_relay = me.z == self.turn
+            self.via = me.seq(me.h, self.turn, me.c)
+        else:
+            self.at_relay = me.z == self.edge
+            self.via = me.seq(row, self.edge, me.c)
+        self.goal = me.seq(row if RELAY == 1 else me.h, self.turn, me.c)
+
+    def copy(self, k, half):
+        nxt = self.me.chip(self.sign)
+        return send(
+            self.at(k - 1, half), self.at(k, half), self.ss.at[half, k - 1], self.rr.at[half, k - 1], nxt, self.me.t
+        )
+
+    def push(self, k):
+        self.copy(k, 0).start()
+
+        @pl.when(self.me.z != self.edge)
+        def _():
+            self.copy(k, 1).start()
+
+        @pl.when(self.me.z == self.edge)
+        def _():
+            send(
+                self.at(k - 1, 1), self.relay.at[k - 1], self.ss.at[1, k - 1], self.rx.at[k - 1], self.via, self.me.t
+            ).start()
+
+    def on(self, k):
+        return send(
+            self.relay.at[k - 1], self.at(k, 1), self.rs.at[k - 1], self.rr.at[1, k - 1], self.goal, self.me.t
+        )
+
+    def take(self, k):
+        @pl.when(self.at_relay)
+        def _():
+            send(
+                self.relay.at[k - 1], self.relay.at[k - 1], self.rs.at[k - 1], self.rx.at[k - 1], self.via, self.me.t
+            ).wait_recv()
+            self.on(k).start()
+
+        for half in (0, 1):
+            self.copy(k, half).wait_recv()
+        if k < 3:
+            self.push(k + 1)
+
+    def finish(self):
+        for k in (1, 2, 3):
+            for half in (0, 1):
+                self.copy(k, half).wait_send()
+
+        @pl.when(self.at_relay)
+        def _():
+            for k in (1, 2, 3):
+                self.on(k).wait_send()
+
+
 def fused_kernel(
-    n_seq, n_ten, delays, text_len, pay, emb, gain, cot, out, de, sgo,
+    n_seq, n_ten, delays, text_len, w_in, t_in, s_in, emb, gain, cot, out, de, sgo,
+    pay, tmp,
     g, f, cots, rimbuf, blk, longer, nst, normed, states32, states,
-    kv, qd, tkv, kx, qx, wbuf, wtbuf, mixbuf, totbuf, st, cstat,
+    tkv, kx, qx, k_relay, q_relay, wbuf, wtbuf, mixbuf, totbuf, st, cstat,
     att, dq, dk, dv, tkg, tvg,
     opt, opx, opr, ipt, ipx, ipr, ops, ips, nst_out, nsx, nss, nsr,
     sga, sgza, sgb, sgzb, sgh, sghr, sgs, sgx, fg, rim,
     lsem, one_s, one_r, h_s, h_r, z_s, z_r, f_s, f_r, x_s, x_r,
-    k_s, k_r, q_s, q_r, t_s, t_r, ox_s, ox_r, ix_s, ix_r, o_s, o_r, i_s, i_r, n_s, n_r,
+    k_s, k_r, k_rs, k_rx, q_s, q_r, q_rs, q_rx, t_s, t_r, ox_s, ox_r, ix_s, ix_r, o_s, o_r, i_s, i_r, n_s, n_r,
     za_s, za_r, zb_s, zb_r, hh_s, hh_r,
 ):
     me = Place(n_seq, n_ten)
@@ -120,6 +183,19 @@
     def half_rows(core):
         return pl.ds(pl.multiple_of(core * Q, Q), Q)
 
+    per = text // n_seq
+    given = t_in[0].shape[0]
+    tmp[...] = jnp.zeros_like(tmp)
+    for i in range(2):
+        tmp[i, 0:given, :] = t_in[i][...].astype(F32)
+        for e in range(2):
+            tmp[i, 12:16, e * 128 : (e + 1) * 128] = s_in[e * 8 + i * 4 : e * 8 + i * 4 + 4, :]
+    for e in range(2):
+        lanes = slice(e * 128, (e + 1) * 128)
+        for i in range(4):
+            pay[e, i * R : (i + 1) * R, :] = w_in[i][:, lanes]
+        for i in range(2):
+            pay[e, 4 * R + 16 * i : 4 * R + 16 * (i + 1), :] = tmp[i, :, lanes].astype(BF)
     go(send(pay.at[1 - c], g.at[p, c], one_s.at[0], one_r.at[0], sib, t))
     mine = pltpu.make_async_copy(pay.at[c], g.at[p, c], lsem.at[0])
     mine.start()
@@ -231,44 +307,29 @@
     def weight(i):
         return g[:, :, i * R : (i + 1) * R, :].reshape(n_seq * R, 128)
 
-    def project(src, i, dst, lanes):
+    def project(src, i, dst, first, lanes):
         def go_rows(rb, carry):
-            rows = half_rows(rb)
-            dst[rows, lanes] = nn(src[rows, :], weight(i)).astype(BF)
+            rows = pl.ds(pl.multiple_of(first + rb * Q, Q), Q)
+            dst[rows, lanes] = nn(src[half_rows(rb), :], weight(i)).astype(BF)
             return carry
 
         lax.fori_loop(0, 2, go_rows, 0)
 
     lo, hi = slice(0, 128), slice(128, 256)
-
-    def kslot(k):
-        return kx.at[pl.ds((3 - k) * B, B)]
-
-    def qslot(k):
-        return qx.at[pl.ds(k * B, B)]
-
-    project(normed, 1, kv, lo)
-    project(normed, 2, kv, hi)
-    go(send(kv, kslot(1), k_s.at[0], k_r.at[0], me.chip(1), t))
-    project(normed, 0, qd, lo)
+    keys = Chain(
+        me, 1, lambda k, e: kx.at[pl.ds((3 - k) * B + e * Q, Q)], k_relay, k_s, k_r, k_rs, k_rx
+    )
+    queries = Chain(me, -1, lambda k, e: qx.at[pl.ds(k * B + e * Q, Q)], q_relay, q_s, q_r, q_rs, q_rx)
+    kv = kx.at[pl.ds(3 * B, B)]
+    qd = qx.at[pl.ds(0, B)]
+    project(normed, 1, kx, 3 * B, lo)
+    project(normed, 2, kx, 3 * B, hi)
+    keys.push(1)
+    project(normed, 0, qx, 0, lo)
     mycot.wait()
     send(cot, cots.at[half_rows(c)], one_s.at[2], one_r.at[2], sib, t).wait_recv()
-    project(cots, 3, qd, hi)
-    go(send(qd, qslot(1), q_s.at[0], q_r.at[0], me.chip(-1), t))
-    kx[pl.ds(3 * B, B), :] = kv[...]
-    qx[pl.ds(0, B), :] = qd[...]
-
-    states32[...] = g[:, :, 4 * R + 32 : 4 * R + 48, :].reshape(n_seq, 16, 128).astype(F32)
-    per = text // n_seq
-    qn = 16 // per
-    for r in range(per):
-        for qq in range(qn):
-            states[r * n_seq : (r + 1) * n_seq, qq * 128 : (qq + 1) * 128] = states32[:, r * qn + qq, :].astype(BF)
-    for i in range(2):
-        w = g[:, :, 4 * R + 16 * i : 4 * R + 16 * (i + 1), :].reshape(n_seq * 16, 128)
-        tkv[:, i * 128 : (i + 1) * 128] = nn(states[...], w).astype(BF)
-    token = lax.broadcasted_iota(jnp.int32, (1, text), 1)
-    live = lax.rem(token, n_seq) * per + lax.div(token, n_seq) < text_len[0]
+    project(cots, 3, qx, 0, hi)
+    queries.push(1)
 
     lane = lax.broadcasted_iota(jnp.int32, (Q, 128), 1)
     row = lax.broadcasted_iota(jnp.int32, (Q, Q), 0)
@@ -295,31 +356,40 @@
             for hd in range(2):
                 q = jnp.where(heads[hd], q_both, zero) * jnp.asarray(scale, BF)
                 if k == 0:
+                    total, mix = jnp.zeros((Q, 128), F32), jnp.zeros((Q, 128), F32)
+                else:
+                    total, mix = totbuf[qb, hd], mixbuf[qb, hd]
+                if k == 4:
                     wt = jnp.where(live, jnp.exp(nt(q, tkv[:, lo])), 0.0)
                     wtbuf[qb, hd] = wt
-                    total, mix = wt, nn(wt.astype(BF), tkv[:, hi])
-                else:
-                    total, mix = totbuf[qb, hd], mixbuf[qb, hd]
+                    total, mix = total + wt, mix + nn(wt.astype(BF), tkv[:, hi])
                 for j in range(chunks):
                     if (qb + j) // 2 == 3 - k:
                         a, b = forward_chunk(qb, hd, q, j)
                         total, mix = total + a, mix + b
                 totbuf[qb, hd], mixbuf[qb, hd] = total, mix
 
-    def pass_keys(k):
-        send(kv, kslot(k), k_s.at[k - 1], k_r.at[k - 1], me.chip(1), t).wait_recv()
-        if k < 3:
-            go(send(kslot(k), kslot(k + 1), k_s.at[k], k_r.at[k], me.chip(1), t))
-
-    def pass_queries(k):
-        send(qd, qslot(k), q_s.at[k - 1], q_r.at[k - 1], me.chip(-1), t).wait_recv()
-        if k < 3:
-            go(send(qslot(k), qslot(k + 1), q_s.at[k], q_r.at[k], me.chip(-1), t))
-
+    states32[...] = g[:, :, 4 * R : 4 * R + 32, :].reshape(n_seq, 32, 128).astype(F32)
+    lanes_of = 8 // (per // 2)
+    for e in range(8):
+        at = 12 + e if e < 4 else 24 + e
+        first = pl.multiple_of((c * (per // 2) + e // lanes_of) * n_seq, n_seq)
+        x = (e % lanes_of) * 128
+        states[pl.ds(first, n_seq), x : x + 128] = states32[:, at, :].astype(BF)
+    my_states = states.at[pl.ds(pl.multiple_of(c * (text // 2), text // 2), text // 2)]
+    go(send(my_states, my_states, one_s.at[5], one_r.at[5], sib, t))
     forward(0)
+    send(my_states, my_states, one_s.at[5], one_r.at[5], sib, t).wait_recv()
+    for i in range(2):
+        w = g[:, :, 4 * R + 16 * i : 4 * R + 16 * (i + 1), :].reshape(n_seq * 16, 128)
+        tkv[:, i * 128 : (i + 1) * 128] = nn(states[...], w).astype(BF)
+    token = lax.broadcasted_iota(jnp.int32, (1, text), 1)
+    live = lax.rem(token, n_seq) * per + lax.div(token, n_seq) < text_len[0]
+
+    forward(4)
     for k in (1, 2, 3):
-        pass_keys(k)
-        pass_queries(k)
+        keys.take(k)
+        queries.take(k)
         forward(k)
     for qb in range(2):
         rows = slice(qb * Q, (qb + 1) * Q)
@@ -380,9 +450,9 @@
             tvg[...] += tn(sh.astype(BF), d)
             for j in range(chunks):
                 base = pl.multiple_of((qb + j) * Q, Q)
-                keys = kx[pl.ds(base, Q), :]
-                ds = (wbuf[qb, hd, j] * r * (nt(d, keys[:, hi]) - inner)).astype(BF)
-                grad = grad + nn(ds, keys[:, lo])
+                around = kx[pl.ds(base, Q), :]
+                ds = (wbuf[qb, hd, j] * r * (nt(d, around[:, hi]) - inner)).astype(BF)
+                grad = grad + nn(ds, around[:, lo])
             parts.append(grad)
         dq[rows, :] = (jnp.where(heads[0], parts[0], parts[1]) * scale).astype(BF)
         return carry
@@ -436,7 +506,7 @@
         dv[rows, :] = jnp.where(heads[0], vparts[0], vparts[1]).astype(BF)
         return carry
 
-    lax.fori_loop(0, 2, key_grads, 0)
+    key_grads(1 - c, 0)
 
     def input_block(cc, tt):
         rows = half_rows(cc)
@@ -462,6 +532,7 @@
         go(send(ipt.at[d], ipx.at[d], ix_s.at[d], ix_r.at[d], sib, t))
     nst_out[...] = pack_sums(plain, unit)
     go(send(nst_out, nsx, n_s.at[0], n_r.at[0], sib, t))
+    key_grads(c, 0)
     plain = jnp.zeros((Q, 128), F32)
     unit = jnp.zeros((Q, 128), F32)
     for d in [*range(1, T), 0]:
@@ -522,21 +593,25 @@
     sgo[:, hi] = jnp.where(c == 0, sgx[...], sgs[c])
     for copy in outgoing:
         copy.wait_send()
+    for chain in (keys, queries):
+        chain.finish()
     longer[Q : Q + 16, :] = jnp.where(s < n_seq - 1, rim[...].astype(F32), 0.0)
+    later = [longer[d : d + Q, :] for d in range(4)]
     for k in range(4):
-        book = jnp.zeros((Q, width), F32)
-        for d in range(4):
-            book = jnp.where(delays[k] == d, longer[d : d + Q, :], book)
+        book = later[0]
+        for d in range(1, 4):
+            book = jnp.where(delays[k] == d, later[d], book)
         de[k] = book.astype(BF)
 
 
-def fused(n_seq, n_ten, delays, text_len, pay, emb, gain, cot, text):
+def fused(n_seq, n_ten, delays, text_len, weights, text_weights, states, emb, gain, cot, text):
     H, Z = dims_of(n_seq)
     T = n_ten
     _, Q, W = emb.shape
     B = 2 * Q
     full = W * T
-    R = (pay.shape[1] - 48) // 4
+    R = weights[0].shape[0]
+    pay_shape = (2, 4 * R + 32, 128)
     chunks = (WINDOW + Q - 2) // Q + 1
     dma = pltpu.SemaphoreType.DMA
     vm = pl.BlockSpec(memory_space=pltpu.VMEM)
@@ -551,19 +626,19 @@
         return [dma(shape), dma(shape)]
 
     return pl.pallas_call(
-        functools.partial(fused_kernel, n_seq, n_ten),
+        lambda a, b, *refs: fused_kernel(n_seq, n_ten, a, b, refs[0:4], refs[4:6], *refs[6:]),
         out_shape=(
             jax.ShapeDtypeStruct((Q, W), BF),
             jax.ShapeDtypeStruct((4, Q, W), BF),
             jax.ShapeDtypeStruct((R + 32, 256), F32),
         ),
-        in_specs=[sm, sm, vm, vm, vm, pl.BlockSpec(memory_space=pl.ANY)],
+        in_specs=[sm, sm] + [vm] * 9 + [pl.BlockSpec(memory_space=pl.ANY)],
         out_specs=(vm,) * 3,
         scratch_shapes=[
-            V((H * Z,) + pay.shape, BF), V((2, T, Q, W), BF), V((B, full), BF), V((16, W), F32), V((Q, W), BF),
-            V((Q + 16, W), F32), V((2, Q, 128), F32), V((B, full), BF), V((n_seq, 16, 128), F32),
+            V(pay_shape, BF), V((2, 16, 256), F32), V((H * Z,) + pay_shape, BF), V((2, T, Q, W), BF), V((B, full), BF), V((16, W), F32), V((Q, W), BF),
+            V((Q + 16, W), F32), V((2, Q, 128), F32), V((B, full), BF), V((n_seq, 32, 128), F32),
             V((text, n_seq * 16), BF),
-            V((B, 256), BF), V((B, 256), BF), V((text, 256), BF), V((4 * B, 256), BF), V((4 * B, 256), BF),
+            V((text, 256), BF), V((4 * B, 256), BF), V((4 * B, 256), BF), V((3, Q, 256), BF), V((3, Q, 256), BF),
             V((2, 2, chunks, Q, Q), F32), V((2, 2, Q, text), F32), V((2, 2, Q, 128), F32), V((2, 2, Q, 128), F32),
             V((4, 8, B), F32), V((B, 128), F32),
             rows, rows, rows, rows, small, small,
@@ -571,12 +646,12 @@
             V((Z, H, 2, R, 128), BF), V((Z, H, 2, R, 128), BF), V((Z, H, 2, 32, 128), BF), V((Z, H, 2, 32, 128), BF),
             V((H, 2, R + 32, 128), F32), V((H, 2, R + 32, 128), F32), V((2, R + 32, 128), F32), V((R + 32, 128), F32),
             V((Q, W), BF), V((16, W), BF),
-            dma((3,)), *pair(5), *pair(H), *pair(2, Z // 2 + 1, H), *pair(T), *pair(T),
-            *pair(3), *pair(3), *pair(4), *pair(T), *pair(T), *pair(T), *pair(T), *pair(T),
+            dma((3,)), *pair(6), *pair(H), *pair(2, Z // 2 + 1, H), *pair(T), *pair(T),
+            *pair(2, 3), *pair(3), *pair(2, 3), *pair(3), *pair(4), *pair(T), *pair(T), *pair(T), *pair(T), *pair(T),
             *pair(Z), *pair(Z), *pair(H),
         ],
         compiler_params=pltpu.CompilerParams(collective_id=0, has_side_effects=True, vmem_limit_bytes=56 << 20),
-    )(delays, text_len, pay, emb, gain, cot)
+    )(delays, text_len, *weights, *text_weights, states, emb, gain, cot)
 
 
 def shards(
@@ -587,13 +662,9 @@
     tr = w_text_key.shape[0]
     per = text_states.shape[0]
     states = jnp.pad(text_states.reshape(per, n_seq, tr), ((0, 0), (0, 0), (0, 16 - tr))).reshape(16, 128)
-    pieces = [w_query, w_key, w_value, w_out.T]
-    pieces += [jnp.pad(w, ((0, 16 - tr), (0, 0))) for w in (w_text_key, w_text_value)]
-    pay = jnp.concatenate(pieces, 0)
-    pay = jnp.stack([jnp.concatenate([pay[:, i * 128 : (i + 1) * 128], states], 0) for i in range(2)], 0)
     out, de, sgo = fused(
-        n_seq, n_ten, delays, text_len, pay, embedded.transpose(1, 0, 2), norm_gain.reshape(1, -1),
-        cotangent, per * n_seq,
+        n_seq, n_ten, delays, text_len, (w_query, w_key, w_value, w_out.T), (w_text_key, w_text_value),
+        states.astype(F32), embedded.transpose(1, 0, 2), norm_gain.reshape(1, -1), cotangent, per * n_seq,
     )
     return (out, de.transpose(1, 0, 2), sgo[:R].T, sgo[R : R + tr], sgo[R + 16 : R + 16 + tr])
 

time: 150 us -> 139 us (0.927)
  the two profiles are of different devices: /device:TPU:201 before, /device:TPU:1 now
where the time goes in v3:
time: 139 us; the launch traced here: 137 us
  Pallas kernels  129 us (93%)
  local copies, waits for them, and re-layouts  6.89 us (5%)
    pallas_call x1, Pallas kernels, fused(): pl.pallas_call(lambda a, b, *refs: fused_kernel(n_seq, n_ten, a, b, refs[...  129 us
    unnamed x9, local copies, waits for them, and re-layouts  4.86 us

profile of v3, /device:TPU:1, one launch (start us, length us, event | category | flops | bytes accessed | tf_op | source)
XLA Modules:
  0.0 136.9 jit_solution(5426549677329760813)
XLA Ops:
  0.6 0.0 copy-start.2
  1.3 0.0 copy-done.2
  1.3 0.1 reshape.19
  1.5 0.7 reshape.21.refs_6_
  2.1 1.9 %copy.22 = bf16[256,4,256]{2,0,1:T(8,128)(2,1)} copy(bf16[256,4,256]{2,1,0:T(4,128)(2,1)} %param.12) | data formatting | bytes 1048576 | tf_op args[0]
  4.0 128.7 %shard_map.155 = (bf16[256,256]{1,0:T(8,128)(2,1)}, bf16[4,256,256]{2,1,0:T(8,128)(2,1)}, f32[64,256]{1,0:T(8,128)}) custom-call(s32[4]{0:T(128)} %a.1, s32[1]{0:T(128)S(6)} %copy.24.b, bf16[32,256]{1,0:T(8,128)(2,1)} %refs_0_.1, bf16[32,256]{1,0:T(8,128)(2,1)} %refs_1_.1, bf16[32,256]{1,0:T(8,128)(2,1)} %refs_2_.1, bf16[32,256]{1,0:T(8,128)(2,1)} %bitcast.10, ...), custom_call_target="tpu_custom_call" | custom-call | tf_op jit(solution)/shard_map/pallas_call | solution.py:628
  132.8 0.0 copy-start.1
  132.8 2.3 %copy.20 = bf16[256,4,256]{2,1,0:T(4,128)(2,1)} copy(bf16[256,4,256]{2,0,1:T(8,128)(2,1)} %bitcast.9) | data formatting | bytes 1048576
  135.0 0.0 copy-done.1
  135.0 0.0 copy-start
  135.0 0.6 slice_bitcast_fusion
  135.7 0.6 fusion
  136.3 0.0 copy-done
  136.3 0.7 copy.25
  (1 shorter events, 0.0 us)
Async XLA Ops:
  0.6 0.7 copy-start.2
  132.8 2.3 %copy-start.1 = (f32[64,256]{1,0:T(8,128)S(1)}, f32[64,256]{1,0:T(8,128)}, u32[]{:S(2)}) copy-start(f32[64,256]{1,0:T(8,128)} %get-tuple-element.10) | copy-start | bytes 196612
  135.0 1.2 copy-start

commit v4 on v3

--- a/solution.py
+++ b/solution.py
@@ -44,7 +44,7 @@
     sem = pltpu.get_barrier_semaphore()
     for seq, ten in partners:
         pl.semaphore_signal(sem, inc=1, device_id=(seq, ten), device_id_type=MESH)
-    pl.semaphore_wait(sem, len(partners))
+    return lambda: pl.semaphore_wait(sem, len(partners))
 
 
 class Place:
@@ -100,8 +100,10 @@
             self.at(k - 1, half), self.at(k, half), self.ss.at[half, k - 1], self.rr.at[half, k - 1], nxt, self.me.t
         )
 
-    def push(self, k):
-        self.copy(k, 0).start()
+    def push(self, k, half):
+        if half == 0:
+            self.copy(k, 0).start()
+            return
 
         @pl.when(self.me.z != self.edge)
         def _():
@@ -118,18 +120,19 @@
             self.relay.at[k - 1], self.at(k, 1), self.rs.at[k - 1], self.rr.at[1, k - 1], self.goal, self.me.t
         )
 
-    def take(self, k):
-        @pl.when(self.at_relay)
-        def _():
-            send(
-                self.relay.at[k - 1], self.relay.at[k - 1], self.rs.at[k - 1], self.rx.at[k - 1], self.via, self.me.t
-            ).wait_recv()
-            self.on(k).start()
-
-        for half in (0, 1):
-            self.copy(k, half).wait_recv()
+    def take(self, k, half):
+        if half == 1:
+
+            @pl.when(self.at_relay)
+            def _():
+                send(
+                    self.relay.at[k - 1], self.relay.at[k - 1], self.rs.at[k - 1], self.rx.at[k - 1], self.via, self.me.t
+                ).wait_recv()
+                self.on(k).start()
+
+        self.copy(k, half).wait_recv()
         if k < 3:
-            self.push(k + 1)
+            self.push(k + 1, half)
 
     def finish(self):
         for k in (1, 2, 3):
@@ -144,7 +147,7 @@
 
 def fused_kernel(
     n_seq, n_ten, delays, text_len, w_in, t_in, s_in, emb, gain, cot, out, de, sgo,
-    pay, tmp,
+    pay, tmp, wide,
     g, f, cots, rimbuf, blk, longer, nst, normed, states32, states,
     tkv, kx, qx, k_relay, q_relay, wbuf, wtbuf, mixbuf, totbuf, st, cstat,
     att, dq, dk, dv, tkg, tvg,
@@ -160,7 +163,7 @@
     sib = me.sibling()
     half = Z // 2
     width = emb.shape[2]
-    Q = emb.shape[1]
+    Q = emb.shape[0]
     B = 2 * Q
     R = sga.shape[3]
     text = states.shape[0]
@@ -173,7 +176,7 @@
     partners += [(me.seq(h, me.other_z(d), c), t) for d in range(1, Z)]
     partners += [(s, me.other_t(d)) for d in range(1, T)]
     partners += [(me.chip(k), t) for k in (1, -1, 2, -2, 3, -3)]
-    greet(partners)
+    all_here = greet(partners)
     outgoing = []
 
     def go(copy):
@@ -186,26 +189,21 @@
     per = text // n_seq
     given = t_in[0].shape[0]
     tmp[...] = jnp.zeros_like(tmp)
+    ours = s_in[...].astype(F32)
     for i in range(2):
         tmp[i, 0:given, :] = t_in[i][...].astype(F32)
         for e in range(2):
-            tmp[i, 12:16, e * 128 : (e + 1) * 128] = s_in[e * 8 + i * 4 : e * 8 + i * 4 + 4, :]
+            tmp[i, 12:16, e * 128 : (e + 1) * 128] = ours[e * 8 + i * 4 : e * 8 + i * 4 + 4, :]
     for e in range(2):
         lanes = slice(e * 128, (e + 1) * 128)
         for i in range(4):
             pay[e, i * R : (i + 1) * R, :] = w_in[i][:, lanes]
         for i in range(2):
             pay[e, 4 * R + 16 * i : 4 * R + 16 * (i + 1), :] = tmp[i, :, lanes].astype(BF)
+    all_here()
     go(send(pay.at[1 - c], g.at[p, c], one_s.at[0], one_r.at[0], sib, t))
     mine = pltpu.make_async_copy(pay.at[c], g.at[p, c], lsem.at[0])
     mine.start()
-    longer[...] = jnp.zeros_like(longer)
-    for d in range(4):
-        book = jnp.zeros((Q, width), F32)
-        for k in range(4):
-            book = book + jnp.where(delays[k] == d, emb[k].astype(F32), 0.0)
-        longer[d : d + Q, :] = longer[d : d + Q, :] + book
-    go(send(longer.at[pl.ds(Q, 16)], rimbuf, one_s.at[1], one_r.at[1], me.next(1), t))
     mine.wait()
     send(pay.at[c], g.at[p, 1 - c], one_s.at[0], one_r.at[0], sib, t).wait_recv()
     for d in range(1, H):
@@ -231,6 +229,20 @@
     for way in (0, 1):
         if used(way, 1, 0):
             step(way, 1, 0)
+    wide[...] = emb[...].astype(F32)
+    longer[...] = jnp.zeros_like(longer)
+    for d in range(4):
+        book = jnp.zeros((Q, width), F32)
+        for k in range(4):
+            book = book + jnp.where(delays[k] == d, wide[:, k, :], 0.0)
+        longer[d : d + Q, :] = longer[d : d + Q, :] + book
+    go(send(longer.at[pl.ds(Q, 16)], rimbuf, one_s.at[1], one_r.at[1], me.next(1), t))
+    for d in range(1, H):
+        hh = me.other_h(H - d)
+        send(g.at[hh * Z + z], g.at[hh * Z + z], h_s.at[d], h_r.at[d], sib, t).wait_recv()
+        for way in (0, 1):
+            if used(way, 1, H - d):
+                step(way, 1, H - d)
     send(longer.at[pl.ds(Q, 16)], rimbuf, one_s.at[1], one_r.at[1], me.next(1), t).wait_recv()
     blk[...] = longer[0:Q, :].astype(BF)
     blk[0:16, :] = (longer[0:16, :] + jnp.where(s > 0, rimbuf[...], 0.0)).astype(BF)
@@ -239,12 +251,6 @@
     go(send(blk, f.at[c, t], x_s.at[0], x_r.at[0], sib, t))
     own = pltpu.make_async_copy(blk, f.at[c, t], lsem.at[1])
     own.start()
-    for d in range(1, H):
-        hh = me.other_h(H - d)
-        send(g.at[hh * Z + z], g.at[hh * Z + z], h_s.at[d], h_r.at[d], sib, t).wait_recv()
-        for way in (0, 1):
-            if used(way, 1, H - d):
-                step(way, 1, H - d)
     go(send(cot, cots.at[half_rows(c)], one_s.at[2], one_r.at[2], sib, t))
     mycot = pltpu.make_async_copy(cot, cots.at[half_rows(c)], lsem.at[2])
     mycot.start()
@@ -324,12 +330,14 @@
     qd = qx.at[pl.ds(0, B)]
     project(normed, 1, kx, 3 * B, lo)
     project(normed, 2, kx, 3 * B, hi)
-    keys.push(1)
+    keys.push(1, 1)
+    keys.push(1, 0)
     project(normed, 0, qx, 0, lo)
     mycot.wait()
     send(cot, cots.at[half_rows(c)], one_s.at[2], one_r.at[2], sib, t).wait_recv()
     project(cots, 3, qx, 0, hi)
-    queries.push(1)
+    queries.push(1, 1)
+    queries.push(1, 0)
 
     lane = lax.broadcasted_iota(jnp.int32, (Q, 128), 1)
     row = lax.broadcasted_iota(jnp.int32, (Q, Q), 0)
@@ -388,8 +396,9 @@
 
     forward(4)
     for k in (1, 2, 3):
-        keys.take(k)
-        queries.take(k)
+        for e in (1, 0):
+            keys.take(k, e)
+            queries.take(k, e)
         forward(k)
     for qb in range(2):
         rows = slice(qb * Q, (qb + 1) * Q)
@@ -601,13 +610,14 @@
         book = later[0]
         for d in range(1, 4):
             book = jnp.where(delays[k] == d, later[d], book)
-        de[k] = book.astype(BF)
+        wide[:, k, :] = book
+    de[...] = wide[...].astype(BF)
 
 
 def fused(n_seq, n_ten, delays, text_len, weights, text_weights, states, emb, gain, cot, text):
     H, Z = dims_of(n_seq)
     T = n_ten
-    _, Q, W = emb.shape
+    Q, _, W = emb.shape
     B = 2 * Q
     full = W * T
     R = weights[0].shape[0]
@@ -629,13 +639,13 @@
         lambda a, b, *refs: fused_kernel(n_seq, n_ten, a, b, refs[0:4], refs[4:6], *refs[6:]),
         out_shape=(
             jax.ShapeDtypeStruct((Q, W), BF),
-            jax.ShapeDtypeStruct((4, Q, W), BF),
+            jax.ShapeDtypeStruct((Q, 4, W), BF),
             jax.ShapeDtypeStruct((R + 32, 256), F32),
         ),
         in_specs=[sm, sm] + [vm] * 9 + [pl.BlockSpec(memory_space=pl.ANY)],
         out_specs=(vm,) * 3,
         scratch_shapes=[
-            V(pay_shape, BF), V((2, 16, 256), F32), V((H * Z,) + pay_shape, BF), V((2, T, Q, W), BF), V((B, full), BF), V((16, W), F32), V((Q, W), BF),
+            V(pay_shape, BF), V((2, 16, 256), F32), V((Q, 4, W), F32), V((H * Z,) + pay_shape, BF), V((2, T, Q, W), BF), V((B, full), BF), V((16, W), F32), V((Q, W), BF),
             V((Q + 16, W), F32), V((2, Q, 128), F32), V((B, full), BF), V((n_seq, 32, 128), F32),
             V((text, n_seq * 16), BF),
             V((text, 256), BF), V((4 * B, 256), BF), V((4 * B, 256), BF), V((3, Q, 256), BF), V((3, Q, 256), BF),
@@ -664,9 +674,9 @@
     states = jnp.pad(text_states.reshape(per, n_seq, tr), ((0, 0), (0, 0), (0, 16 - tr))).reshape(16, 128)
     out, de, sgo = fused(
         n_seq, n_ten, delays, text_len, (w_query, w_key, w_value, w_out.T), (w_text_key, w_text_value),
-        states.astype(F32), embedded.transpose(1, 0, 2), norm_gain.reshape(1, -1), cotangent, per * n_seq,
+        states, embedded, norm_gain.reshape(1, -1), cotangent, per * n_seq,
     )
-    return (out, de.transpose(1, 0, 2), sgo[:R].T, sgo[R : R + tr], sgo[R + 16 : R + 16 + tr])
+    return (out, de, sgo[:R].T, sgo[R : R + tr], sgo[R + 16 : R + 16 + tr])
 
 
 def solution(mesh):

time: 139 us -> 142 us (1.022); the launches traced: 137 us -> 141 us
  Pallas kernels: 129 us -> 134 us
    pallas_call x1, Pallas kernels: 129 us -> 134 us  [fused(): pl.pallas_call(lambda a, b, *refs: fused_kernel(n_seq, n_ten, a, b, refs[...]
    unnamed x9 -> x6, local copies, waits for them, and re-layouts: 4.86 us -> 2.69 us
where the time goes in v4:
time: 142 us; the launch traced here: 141 us
  Pallas kernels  134 us (94%)
  local copies, waits for them, and re-layouts  6.26 us (4%)
    pallas_call x1, Pallas kernels, fused(): pl.pallas_call(lambda a, b, *refs: fused_kernel(n_seq, n_ten, a, b, refs[...  134 us

profile of v4, /device:TPU:1, one launch (start us, length us, event | category | flops | bytes accessed | tf_op | source)
XLA Modules:
  0.0 141.4 jit_solution(2915114564441581905)
XLA Ops:
  0.6 0.0 copy-start.1
  1.3 0.0 copy-done.1
  1.3 0.1 reshape.19
  1.5 0.7 reshape.20.refs_6_
  2.1 133.8 %shard_map.155 = (bf16[256,256]{1,0:T(8,128)(2,1)}, bf16[256,4,256]{2,1,0:T(4,128)(2,1)}, f32[64,256]{1,0:T(8,128)}) custom-call(s32[4]{0:T(128)} %a.1, s32[1]{0:T(128)S(6)} %copy.19.b, bf16[32,256]{1,0:T(8,128)(2,1)} %refs_0_.1, bf16[32,256]{1,0:T(8,128)(2,1)} %refs_1_.1, bf16[32,256]{1,0:T(8,128)(2,1)} %refs_2_.1, bf16[32,256]{1,0:T(8,128)(2,1)} %bitcast.4, ...), custom_call_target="tpu_custom_call" | custom-call | tf_op jit(solution)/shard_map/pallas_call | solution.py:638
  136.0 0.0 copy-start
  136.0 1.4 slice_bitcast_fusion
  137.4 1.3 fusion
  138.8 0.0 copy-done
  138.8 0.7 copy.20
  139.4 2.0 %copy.21 = bf16[256,4,256]{2,1,0:T(4,128)(2,1)} copy(bf16[256,4,256]{2,1,0:T(4,128)(2,1)} %get-tuple-element.19) | data formatting | bytes 1048576
  (1 shorter events, 0.0 us)
Async XLA Ops:
  0.6 0.7 copy-start.1
  136.0 2.8 %copy-start = (bf16[256,256]{1,0:T(8,128)(2,1)S(1)}, bf16[256,256]{1,0:T(8,128)(2,1)}, u32[]{:S(2)}) copy-start(bf16[256,256]{1,0:T(8,128)(2,1)} %get-tuple-element.18) | copy-start | bytes 393220

commit v5 on v3

--- a/solution.py
+++ b/solution.py
@@ -144,7 +144,7 @@
 
 def fused_kernel(
     n_seq, n_ten, delays, text_len, w_in, t_in, s_in, emb, gain, cot, out, de, sgo,
-    pay, tmp,
+    pay, tmp, sums_p, sums_u,
     g, f, cots, rimbuf, blk, longer, nst, normed, states32, states,
     tkv, kx, qx, k_relay, q_relay, wbuf, wtbuf, mixbuf, totbuf, st, cstat,
     att, dq, dk, dv, tkg, tvg,
@@ -474,16 +474,26 @@
     for k in (1, 2, 3):
         send(st.at[0], st.at[k], t_s.at[k], t_r.at[k], me.chip(-k), t).wait_recv()
 
-    def key_grads(kb, carry):
-        rows = half_rows(kb)
+    K = Q // 2
+
+    def quarter(kb, e):
+        return pl.ds(pl.multiple_of(kb * Q + e * K, K), K)
+
+    krow = lax.broadcasted_iota(jnp.int32, (K, Q), 0)
+    qcol = lax.broadcasted_iota(jnp.int32, (K, Q), 1)
+    klane = lax.broadcasted_iota(jnp.int32, (K, 128), 1)
+    kheads = [klane < HD, klane >= HD]
+
+    def key_grads(kb, e):
+        rows = quarter(kb, e)
         k_both = kv[rows, lo]
         v_both = kv[rows, hi]
         kparts, vparts = [], []
         for hd in range(2):
-            kh = jnp.where(heads[hd], k_both, zero) * jnp.asarray(scale, BF)
-            vh = jnp.where(heads[hd], v_both, zero)
-            gk = jnp.zeros((Q, 128), F32)
-            gv = jnp.zeros((Q, 128), F32)
+            kh = jnp.where(kheads[hd], k_both, zero) * jnp.asarray(scale, BF)
+            vh = jnp.where(kheads[hd], v_both, zero)
+            gk = jnp.zeros((K, 128), F32)
+            gv = jnp.zeros((K, 128), F32)
             for i in range(chunks):
                 base = pl.multiple_of((kb + i) * Q, Q)
                 qs = qx[pl.ds(base, Q), :]
@@ -493,58 +503,68 @@
                 inner = st[at, 2 + hd : 3 + hd, part]
                 ok = p * B + (kb + i) * Q < n_seq * Q
                 if i == 0:
-                    ok = ok & (col >= row)
-                if i * Q + Q - 1 >= WINDOW:
-                    ok = ok & (i * Q + col - row < WINDOW)
+                    ok = ok & (qcol >= e * K + krow)
+                if i * Q + Q - 1 - e * K >= WINDOW:
+                    ok = ok & (i * Q + qcol - (e * K + krow) < WINDOW)
                 sh = jnp.where(ok, jnp.exp(nt(kh, qs[:, lo])) * r, 0.0)
                 ds = (sh * (nt(vh, qs[:, hi]) - inner)).astype(BF)
                 gv = gv + nn(sh.astype(BF), qs[:, hi])
                 gk = gk + nn(ds, qs[:, lo])
             kparts.append(gk)
             vparts.append(gv)
-        dk[rows, :] = (jnp.where(heads[0], kparts[0], kparts[1]) * scale).astype(BF)
-        dv[rows, :] = jnp.where(heads[0], vparts[0], vparts[1]).astype(BF)
-        return carry
-
-    key_grads(1 - c, 0)
-
-    def input_block(cc, tt):
-        rows = half_rows(cc)
+        dk[rows, :] = (jnp.where(kheads[0], kparts[0], kparts[1]) * scale).astype(BF)
+        dv[rows, :] = jnp.where(kheads[0], vparts[0], vparts[1]).astype(BF)
+
+    def input_block(cc, e, tt):
+        rows = quarter(cc, e)
         grad = nt(dq[rows, :], w_block(0, tt)) + nt(dk[rows, :], w_block(1, tt)) + nt(dv[rows, :], w_block(2, tt))
         lanes = pl.ds(pl.multiple_of(tt * width, width), width)
+        here = slice(e * K, (e + 1) * K)
         scaled = grad * gain[0:1, lanes]
-        unit = (f[cc, tt].astype(F32) - nst[cc, :, 0:1]) * nst[cc, :, 1:2]
+        unit = (f[cc, tt, here, :].astype(F32) - nst[cc, here, 0:1]) * nst[cc, here, 1:2]
         both = scaled * unit
         return grad, scaled[:, 0:128] + scaled[:, 128:256], both[:, 0:128] + both[:, 128:256]
 
-    def pack_sums(plain, unit):
-        plain = jnp.sum(plain, 1, keepdims=True)
-        unit = jnp.sum(unit, 1, keepdims=True)
+    def pack_sums(which):
+        plain = jnp.sum(sums_p[which], 1, keepdims=True)
+        unit = jnp.sum(sums_u[which], 1, keepdims=True)
         return jnp.where(lane == 0, plain, unit).T[0:8, :]
 
-    plain = jnp.zeros((Q, 128), F32)
-    unit = jnp.zeros((Q, 128), F32)
-    for d in [*range(1, T), 0]:
-        tt = me.other_t(d)
-        grad, a, b = input_block(1 - c, tt)
-        plain, unit = plain + a, unit + b
-        ipt[d] = grad.astype(BF)
-        go(send(ipt.at[d], ipx.at[d], ix_s.at[d], ix_r.at[d], sib, t))
-    nst_out[...] = pack_sums(plain, unit)
-    go(send(nst_out, nsx, n_s.at[0], n_r.at[0], sib, t))
-    key_grads(c, 0)
-    plain = jnp.zeros((Q, 128), F32)
-    unit = jnp.zeros((Q, 128), F32)
-    for d in [*range(1, T), 0]:
-        tt = me.other_t(d)
-        grad, a, b = input_block(c, tt)
-        plain, unit = plain + a, unit + b
-        send(ipt.at[d], ipx.at[d], ix_s.at[d], ix_r.at[d], sib, t).wait_recv()
-        ips[d] = (grad + ipx[d].astype(F32)).astype(BF)
-        if d:
-            go(send(ips.at[d], ipr.at[d], i_s.at[d], i_r.at[d], s, tt))
+    def to_sib(d, e):
+        rows = pl.ds(e * K, K)
+        return send(ipt.at[d, rows], ipx.at[d, rows], ix_s.at[d, e], ix_r.at[d, e], sib, t)
+
+    def to_owner(d, e):
+        rows = pl.ds(e * K, K)
+        return send(ips.at[d, rows], ipr.at[d, rows], i_s.at[d, e], i_r.at[d, e], s, me.other_t(d))
+
+    for e in range(2):
+        here = slice(e * K, (e + 1) * K)
+        key_grads(1 - c, e)
+        plain = jnp.zeros((K, 128), F32)
+        unit = jnp.zeros((K, 128), F32)
+        for d in [*range(1, T), 0]:
+            grad, a, b = input_block(1 - c, e, me.other_t(d))
+            plain, unit = plain + a, unit + b
+            ipt[d, here, :] = grad.astype(BF)
+            go(to_sib(d, e))
+        sums_p[0, here, :], sums_u[0, here, :] = plain, unit
+        if e == 1:
+            nst_out[...] = pack_sums(0)
+            go(send(nst_out, nsx, n_s.at[0], n_r.at[0], sib, t))
+        key_grads(c, e)
+        plain = jnp.zeros((K, 128), F32)
+        unit = jnp.zeros((K, 128), F32)
+        for d in [*range(1, T), 0]:
+            grad, a, b = input_block(c, e, me.other_t(d))
+            plain, unit = plain + a, unit + b
+            to_sib(d, e).wait_recv()
+            ips[d, here, :] = (grad + ipx[d, here, :].astype(F32)).astype(BF)
+            if d:
+                go(to_owner(d, e))
+        sums_p[1, here, :], sums_u[1, here, :] = plain, unit
     send(nst_out, nsx, n_s.at[0], n_r.at[0], sib, t).wait_recv()
-    nss[...] = pack_sums(plain, unit) + nsx[...]
+    nss[...] = pack_sums(1) + nsx[...]
     for d in range(1, T):
         go(send(nss, nsr.at[d], n_s.at[d], n_r.at[d], s, me.other_t(d)))
 
@@ -566,7 +586,8 @@
     for d in range(1, T):
         send(nss, nsr.at[d], n_s.at[d], n_r.at[d], sib, t).wait_recv()
         sums = sums + nsr[d]
-        send(ips.at[d], ipr.at[d], i_s.at[d], i_r.at[d], sib, t).wait_recv()
+        to_owner(d, 0).wait_recv()
+        to_owner(d, 1).wait_recv()
         total = total + ipr[d].astype(F32)
     tall = jnp.concatenate([sums] * 16, 0).T
     here = pl.ds(pl.multiple_of(t * width, width), width)
@@ -635,7 +656,7 @@
         in_specs=[sm, sm] + [vm] * 9 + [pl.BlockSpec(memory_space=pl.ANY)],
         out_specs=(vm,) * 3,
         scratch_shapes=[
-            V(pay_shape, BF), V((2, 16, 256), F32), V((H * Z,) + pay_shape, BF), V((2, T, Q, W), BF), V((B, full), BF), V((16, W), F32), V((Q, W), BF),
+            V(pay_shape, BF), V((2, 16, 256), F32), V((2, Q, 128), F32), V((2, Q, 128), F32), V((H * Z,) + pay_shape, BF), V((2, T, Q, W), BF), V((B, full), BF), V((16, W), F32), V((Q, W), BF),
             V((Q + 16, W), F32), V((2, Q, 128), F32), V((B, full), BF), V((n_seq, 32, 128), F32),
             V((text, n_seq * 16), BF),
             V((text, 256), BF), V((4 * B, 256), BF), V((4 * B, 256), BF), V((3, Q, 256), BF), V((3, Q, 256), BF),
@@ -647,7 +668,7 @@
             V((H, 2, R + 32, 128), F32), V((H, 2, R + 32, 128), F32), V((2, R + 32, 128), F32), V((R + 32, 128), F32),
             V((Q, W), BF), V((16, W), BF),
             dma((3,)), *pair(6), *pair(H), *pair(2, Z // 2 + 1, H), *pair(T), *pair(T),
-            *pair(2, 3), *pair(3), *pair(2, 3), *pair(3), *pair(4), *pair(T), *pair(T), *pair(T), *pair(T), *pair(T),
+            *pair(2, 3), *pair(3), *pair(2, 3), *pair(3), *pair(4), *pair(T), *pair(T, 2), *pair(T), *pair(T, 2), *pair(T),
             *pair(Z), *pair(Z), *pair(H),
         ],
         compiler_params=pltpu.CompilerParams(collective_id=0, has_side_effects=True, vmem_limit_bytes=56 << 20),

time: 139 us -> 141 us (1.014)
  the two profiles are of different devices: /device:TPU:1 before, /device:TPU:195 now
where the time goes in v5:
time: 141 us
  Pallas kernels  133 us (94%)
  local copies, waits for them, and re-layouts  6.89 us (5%)
    pallas_call x1, Pallas kernels, fused(): pl.pallas_call(lambda a, b, *refs: fused_kernel(n_seq, n_ten, a, b, refs[...  133 us
    unnamed x9, local copies, waits for them, and re-layouts  4.86 us

profile of v5, /device:TPU:195, one launch (start us, length us, event | category | flops | bytes accessed | tf_op | source)
XLA Modules:
  0.0 140.8 jit_solution(9318148380146113271)
XLA Ops:
  0.6 0.0 copy-start.2
  1.3 0.0 copy-done.2
  1.3 0.1 reshape.19
  1.5 0.7 reshape.21.refs_6_
  2.1 1.9 %copy.22 = bf16[256,4,256]{2,0,1:T(8,128)(2,1)} copy(bf16[256,4,256]{2,1,0:T(4,128)(2,1)} %param.12) | data formatting | bytes 1048576 | tf_op args[0]
  4.0 132.6 %shard_map.155 = (bf16[256,256]{1,0:T(8,128)(2,1)}, bf16[4,256,256]{2,1,0:T(8,128)(2,1)}, f32[64,256]{1,0:T(8,128)}) custom-call(s32[4]{0:T(128)} %a.1, s32[1]{0:T(128)S(6)} %copy.24.b, bf16[32,256]{1,0:T(8,128)(2,1)} %refs_0_.1, bf16[32,256]{1,0:T(8,128)(2,1)} %refs_1_.1, bf16[32,256]{1,0:T(8,128)(2,1)} %refs_2_.1, bf16[32,256]{1,0:T(8,128)(2,1)} %bitcast.10, ...), custom_call_target="tpu_custom_call" | custom-call | tf_op jit(solution)/shard_map/pallas_call | solution.py:649
  136.6 0.0 copy-start.1
  136.6 2.3 %copy.20 = bf16[256,4,256]{2,1,0:T(4,128)(2,1)} copy(bf16[256,4,256]{2,0,1:T(8,128)(2,1)} %bitcast.9) | data formatting | bytes 1048576
  138.9 0.0 copy-done.1
  138.9 0.0 copy-start
  138.9 0.6 slice_bitcast_fusion
  139.5 0.6 fusion
  140.2 0.0 copy-done
  140.2 0.7 copy.25
  (1 shorter events, 0.0 us)
Async XLA Ops:
  0.6 0.7 copy-start.2
  136.6 2.3 %copy-start.1 = (f32[64,256]{1,0:T(8,128)S(1)}, f32[64,256]{1,0:T(8,128)}, u32[]{:S(2)}) copy-start(f32[64,256]{1,0:T(8,128)} %get-tuple-element.10) | copy-start | bytes 196612
  138.9 1.2 copy-start

commit v6 on v4

--- a/solution.py
+++ b/solution.py
@@ -147,7 +147,7 @@
 
 def fused_kernel(
     n_seq, n_ten, delays, text_len, w_in, t_in, s_in, emb, gain, cot, out, de, sgo,
-    pay, tmp, wide,
+    pay, tmp,
     g, f, cots, rimbuf, blk, longer, nst, normed, states32, states,
     tkv, kx, qx, k_relay, q_relay, wbuf, wtbuf, mixbuf, totbuf, st, cstat,
     att, dq, dk, dv, tkg, tvg,
@@ -163,7 +163,7 @@
     sib = me.sibling()
     half = Z // 2
     width = emb.shape[2]
-    Q = emb.shape[0]
+    Q = emb.shape[1]
     B = 2 * Q
     R = sga.shape[3]
     text = states.shape[0]
@@ -189,11 +189,10 @@
     per = text // n_seq
     given = t_in[0].shape[0]
     tmp[...] = jnp.zeros_like(tmp)
-    ours = s_in[...].astype(F32)
     for i in range(2):
         tmp[i, 0:given, :] = t_in[i][...].astype(F32)
         for e in range(2):
-            tmp[i, 12:16, e * 128 : (e + 1) * 128] = ours[e * 8 + i * 4 : e * 8 + i * 4 + 4, :]
+            tmp[i, 12:16, e * 128 : (e + 1) * 128] = s_in[e * 8 + i * 4 : e * 8 + i * 4 + 4, :]
     for e in range(2):
         lanes = slice(e * 128, (e + 1) * 128)
         for i in range(4):
@@ -229,12 +228,11 @@
     for way in (0, 1):
         if used(way, 1, 0):
             step(way, 1, 0)
-    wide[...] = emb[...].astype(F32)
     longer[...] = jnp.zeros_like(longer)
     for d in range(4):
         book = jnp.zeros((Q, width), F32)
         for k in range(4):
-            book = book + jnp.where(delays[k] == d, wide[:, k, :], 0.0)
+            book = book + jnp.where(delays[k] == d, emb[k].astype(F32), 0.0)
         longer[d : d + Q, :] = longer[d : d + Q, :] + book
     go(send(longer.at[pl.ds(Q, 16)], rimbuf, one_s.at[1], one_r.at[1], me.next(1), t))
     for d in range(1, H):
@@ -610,14 +608,13 @@
         book = later[0]
         for d in range(1, 4):
             book = jnp.where(delays[k] == d, later[d], book)
-        wide[:, k, :] = book
-    de[...] = wide[...].astype(BF)
+        de[k] = book.astype(BF)
 
 
 def fused(n_seq, n_ten, delays, text_len, weights, text_weights, states, emb, gain, cot, text):
     H, Z = dims_of(n_seq)
     T = n_ten
-    Q, _, W = emb.shape
+    _, Q, W = emb.shape
     B = 2 * Q
     full = W * T
     R = weights[0].shape[0]
@@ -639,13 +636,13 @@
         lambda a, b, *refs: fused_kernel(n_seq, n_ten, a, b, refs[0:4], refs[4:6], *refs[6:]),
         out_shape=(
             jax.ShapeDtypeStruct((Q, W), BF),
-            jax.ShapeDtypeStruct((Q, 4, W), BF),
+            jax.ShapeDtypeStruct((4, Q, W), BF),
             jax.ShapeDtypeStruct((R + 32, 256), F32),
         ),
         in_specs=[sm, sm] + [vm] * 9 + [pl.BlockSpec(memory_space=pl.ANY)],
         out_specs=(vm,) * 3,
         scratch_shapes=[
-            V(pay_shape, BF), V((2, 16, 256), F32), V((Q, 4, W), F32), V((H * Z,) + pay_shape, BF), V((2, T, Q, W), BF), V((B, full), BF), V((16, W), F32), V((Q, W), BF),
+            V(pay_shape, BF), V((2, 16, 256), F32), V((H * Z,) + pay_shape, BF), V((2, T, Q, W), BF), V((B, full), BF), V((16, W), F32), V((Q, W), BF),
             V((Q + 16, W), F32), V((2, Q, 128), F32), V((B, full), BF), V((n_seq, 32, 128), F32),
             V((text, n_seq * 16), BF),
             V((text, 256), BF), V((4 * B, 256), BF), V((4 * B, 256), BF), V((3, Q, 256), BF), V((3, Q, 256), BF),
@@ -674,9 +671,9 @@
     states = jnp.pad(text_states.reshape(per, n_seq, tr), ((0, 0), (0, 0), (0, 16 - tr))).reshape(16, 128)
     out, de, sgo = fused(
         n_seq, n_ten, delays, text_len, (w_query, w_key, w_value, w_out.T), (w_text_key, w_text_value),
-        states, embedded, norm_gain.reshape(1, -1), cotangent, per * n_seq,
+        states.astype(F32), embedded.transpose(1, 0, 2), norm_gain.reshape(1, -1), cotangent, per * n_seq,
     )
-    return (out, de, sgo[:R].T, sgo[R : R + tr], sgo[R + 16 : R + 16 + tr])
+    return (out, de.transpose(1, 0, 2), sgo[:R].T, sgo[R : R + tr], sgo[R + 16 : R + 16 + tr])
 
 
 def solution(mesh):

time: 142 us -> 141 us (level)
    unnamed x6 -> x9, local copies, waits for them, and re-layouts: 2.69 us -> 4.86 us
where the time goes in v6:
time: 141 us
  Pallas kernels  133 us (94%)
  local copies, waits for them, and re-layouts  6.89 us (5%)
    pallas_call x1, Pallas kernels, fused(): pl.pallas_call(lambda a, b, *refs: fused_kernel(n_seq, n_ten, a, b, refs[...  133 us
    unnamed x9, local copies, waits for them, and re-layouts  4.86 us

profile of v6, /device:TPU:1, one launch (start us, length us, event | category | flops | bytes accessed | tf_op | source)
XLA Modules:
  0.0 141.0 jit_solution(14499308344580978099)
XLA Ops:
  0.6 0.0 copy-start.2
  1.3 0.0 copy-done.2
  1.3 0.1 reshape.19
  1.5 0.7 reshape.21.refs_6_
  2.1 1.9 %copy.22 = bf16[256,4,256]{2,0,1:T(8,128)(2,1)} copy(bf16[256,4,256]{2,1,0:T(4,128)(2,1)} %param.12) | data formatting | bytes 1048576 | tf_op args[0]
  4.0 132.8 %shard_map.155 = (bf16[256,256]{1,0:T(8,128)(2,1)}, bf16[4,256,256]{2,1,0:T(8,128)(2,1)}, f32[64,256]{1,0:T(8,128)}) custom-call(s32[4]{0:T(128)} %a.1, s32[1]{0:T(128)S(6)} %copy.24.b, bf16[32,256]{1,0:T(8,128)(2,1)} %refs_0_.1, bf16[32,256]{1,0:T(8,128)(2,1)} %refs_1_.1, bf16[32,256]{1,0:T(8,128)(2,1)} %refs_2_.1, bf16[32,256]{1,0:T(8,128)(2,1)} %bitcast.10, ...), custom_call_target="tpu_custom_call" | custom-call | tf_op jit(solution)/shard_map/pallas_call | solution.py:635
  136.8 0.0 copy-start.1
  136.8 2.3 %copy.20 = bf16[256,4,256]{2,1,0:T(4,128)(2,1)} copy(bf16[256,4,256]{2,0,1:T(8,128)(2,1)} %bitcast.9) | data formatting | bytes 1048576
  139.1 0.0 copy-done.1
  139.1 0.0 copy-start
  139.1 0.6 slice_bitcast_fusion
  139.7 0.6 fusion
  140.4 0.0 copy-done
  140.4 0.7 copy.25
  (1 shorter events, 0.0 us)
Async XLA Ops:
  0.6 0.7 copy-start.2
  136.8 2.3 %copy-start.1 = (f32[64,256]{1,0:T(8,128)S(1)}, f32[64,256]{1,0:T(8,128)}, u32[]{:S(2)}) copy-start(f32[64,256]{1,0:T(8,128)} %get-tuple-element.10) | copy-start | bytes 196612
  139.1 1.2 copy-start

commit v7 on v3

--- a/solution.py
+++ b/solution.py
@@ -548,19 +548,6 @@
     for d in range(1, T):
         go(send(nss, nsr.at[d], n_s.at[d], n_r.at[d], s, me.other_t(d)))
 
-    acc_a = sga[z].astype(F32)
-    acc_b = sgb[z].astype(F32)
-    for d in range(1, Z):
-        send(sga.at[0], sgza.at[d], za_s.at[d], za_r.at[d], sib, t).wait_recv()
-        send(sgb.at[0], sgzb.at[d], zb_s.at[d], zb_r.at[d], sib, t).wait_recv()
-        acc_a = acc_a + sgza[d].astype(F32)
-        acc_b = acc_b + sgzb[d].astype(F32)
-    sgh[:, :, 0:R, :] = acc_a
-    sgh[:, :, R : R + 32, :] = acc_b
-    for d in range(1, H):
-        hh = me.other_h(d)
-        go(send(sgh.at[hh], sghr.at[d], hh_s.at[d], hh_r.at[d], me.seq(hh, z, c), t))
-
     total = ips[0].astype(F32)
     sums = nss[...]
     for d in range(1, T):
@@ -575,6 +562,19 @@
     grad = inv * (total * gain[0:1, here] - tall[:, 0:1] / full - unit * (tall[:, 1:2] / full))
     fg[...] = grad.astype(BF)
     go(send(fg.at[pl.ds(0, 16)], rim, one_s.at[3], one_r.at[3], me.next(-1), t))
+
+    acc_a = sga[z].astype(F32)
+    acc_b = sgb[z].astype(F32)
+    for d in range(1, Z):
+        send(sga.at[0], sgza.at[d], za_s.at[d], za_r.at[d], sib, t).wait_recv()
+        send(sgb.at[0], sgzb.at[d], zb_s.at[d], zb_r.at[d], sib, t).wait_recv()
+        acc_a = acc_a + sgza[d].astype(F32)
+        acc_b = acc_b + sgzb[d].astype(F32)
+    sgh[:, :, 0:R, :] = acc_a
+    sgh[:, :, R : R + 32, :] = acc_b
+    for d in range(1, H):
+        hh = me.other_h(d)
+        go(send(sgh.at[hh], sghr.at[d], hh_s.at[d], hh_r.at[d], me.seq(hh, z, c), t))
     acc = sgh[h]
     for d in range(1, H):
         send(sgh.at[0], sghr.at[d], hh_s.at[d], hh_r.at[d], sib, t).wait_recv()

time: 139 us -> 143 us (1.029)
  the two profiles are of different devices: /device:TPU:1 before, /device:TPU:209 now
where the time goes in v7:
time: 143 us
  Pallas kernels  134 us (94%)
  local copies, waits for them, and re-layouts  6.89 us (5%)
    pallas_call x1, Pallas kernels, fused(): pl.pallas_call(lambda a, b, *refs: fused_kernel(n_seq, n_ten, a, b, refs[...  134 us
    unnamed x9, local copies, waits for them, and re-layouts  4.86 us

profile of v7, /device:TPU:209, one launch (start us, length us, event | category | flops | bytes accessed | tf_op | source)
XLA Modules:
  0.0 142.5 jit_solution(3559914577258166624)
XLA Ops:
  0.6 0.0 copy-start.2
  1.3 0.0 copy-done.2
  1.3 0.1 reshape.19
  1.5 0.7 reshape.21.refs_6_
  2.1 1.9 %copy.22 = bf16[256,4,256]{2,0,1:T(8,128)(2,1)} copy(bf16[256,4,256]{2,1,0:T(4,128)(2,1)} %param.12) | data formatting | bytes 1048576 | tf_op args[0]
  4.0 134.3 %shard_map.155 = (bf16[256,256]{1,0:T(8,128)(2,1)}, bf16[4,256,256]{2,1,0:T(8,128)(2,1)}, f32[64,256]{1,0:T(8,128)}) custom-call(s32[4]{0:T(128)} %a.1, s32[1]{0:T(128)S(6)} %copy.24.b, bf16[32,256]{1,0:T(8,128)(2,1)} %refs_0_.1, bf16[32,256]{1,0:T(8,128)(2,1)} %refs_1_.1, bf16[32,256]{1,0:T(8,128)(2,1)} %refs_2_.1, bf16[32,256]{1,0:T(8,128)(2,1)} %bitcast.10, ...), custom_call_target="tpu_custom_call" | custom-call | tf_op jit(solution)/shard_map/pallas_call | solution.py:628
  138.4 0.0 copy-start.1
  138.4 2.3 %copy.20 = bf16[256,4,256]{2,1,0:T(4,128)(2,1)} copy(bf16[256,4,256]{2,0,1:T(8,128)(2,1)} %bitcast.9) | data formatting | bytes 1048576
  140.6 0.0 copy-done.1
  140.6 0.0 copy-start
  140.6 0.6 slice_bitcast_fusion
  141.3 0.6 fusion
  141.9 0.0 copy-done
  141.9 0.7 copy.25
  (1 shorter events, 0.0 us)
Async XLA Ops:
  0.6 0.7 copy-start.2
  138.4 2.3 %copy-start.1 = (f32[64,256]{1,0:T(8,128)S(1)}, f32[64,256]{1,0:T(8,128)}, u32[]{:S(2)}) copy-start(f32[64,256]{1,0:T(8,128)} %get-tuple-element.10) | copy-start | bytes 196612
  140.6 1.2 copy-start
